TPU v7x, 512 devices: a whole 4x8x8 slice. The times are simulated.
512 devices in a mesh: dp: 2 (over core), ctx: 32 (over z, y_hi), tp: 8 (over x, y_lo).
Axes of the slice: x: 4, y: 8 (y_hi: 4, y_lo: 2; y = y_hi * 2 + y_lo), z: 8, core: 2. Of those that a mesh axis runs over, the one named last changes fastest.
Arguments:
- tokens: bfloat16 [32768, 4096], P(('dp', 'ctx')), parts along dimension 0, may hold values from -6 to 6
- lengths: int32 [128], P('dp'), parts along dimension 0, may hold values from 1 to 1537, 16384 in all
- q_weight: bfloat16 [4096, 8, 512], P('ctx', 'tp'), may hold values from -1 to 1
- kv_weight: bfloat16 [4096, 8, 256], P('ctx', 'tp'), may hold values from -1 to 1
Outputs:
- context: bfloat16 [32768, 8, 512], P(('dp', 'ctx'), 'tp'), parts along dimension 0
There are 2 independent parts, one for each index of `dp`. A program takes and returns all parts, laid end to end along the dimension named above; an argument that names none is the same for every part. Nothing has to cross between parts.
Inputs may be any that keep to these rules, and one draw needn't show every extreme that they name: The lengths sum to 16384 and the longest is exactly 1537.
All inputs are finite; a program needn't handle non-finite values.
Results may differ from a plain program's by a relative error of at most 0.0064.
Values may be sent and summed in bfloat16 or wider, within the bound.
No kernel may reach another device: no remote copies, remote signals or barrier semaphores. Data moves between devices by JAX's collectives and lax.ppermute only.
A program may use at most 128 MiB of HBM per device.

v0:
```python
import math

import jax
import jax.numpy as jnp
from jax import lax
from jax.sharding import PartitionSpec as P

masked_score = -1e30


def shifted(value, axis, steps):
    count = lax.axis_size(axis)
    first, last = (max(0, -steps), min(count, count - steps))
    return lax.ppermute(value, axis, [(source, source + steps) for source in range(first, last)])


def rotate(values, positions):
    half = values.shape[-1] // 2
    freqs = jnp.exp(
        jnp.arange(half, dtype=jnp.float32) * (-2.0 * math.log(500000.0) / values.shape[-1])
    )
    angle = positions.astype(jnp.float32)[:, None] * freqs[None, :]
    cosine = jnp.cos(angle)[:, None, None, :]
    sine = jnp.sin(angle)[:, None, None, :]
    first = values[..., :half]
    second = values[..., half:]
    return jnp.concatenate(
        [first * cosine - second * sine, second * cosine + first * sine], axis=-1
    )


def document_of(positions, doc_ends):
    return jnp.sum((positions[:, None] >= doc_ends[None, :]).astype(jnp.int32), axis=1)


def per_device(tokens, lengths, q_weight, kv_weight):
    rows = tokens.shape[0]
    head_dim = kv_weight.shape[2] // 2
    q_cols = q_weight.shape[2]
    heads = q_cols // head_dim
    shard = lax.axis_index("ctx")

    def project(piece):
        return jnp.dot(
            tokens, piece.reshape(piece.shape[0], -1), preferred_element_type=jnp.float32
        )

    q_sum = project(lax.all_gather(q_weight, "ctx", axis=0, tiled=True))
    kv_sum = project(lax.all_gather(kv_weight, "ctx", axis=0, tiled=True))
    positions = shard * rows + jnp.arange(rows, dtype=jnp.int32)
    queries = rotate(q_sum.reshape(rows, 1, heads, head_dim), positions).astype(jnp.bfloat16)
    keys = rotate(kv_sum[:, None, None, :head_dim], positions)[:, :, 0, :].astype(jnp.bfloat16)
    own_block = jnp.concatenate([keys, kv_sum[:, None, head_dim:].astype(jnp.bfloat16)], axis=-1)
    earlier = []
    for distance in range(3, 0, -1):
        earlier.append(shifted(own_block, "ctx", distance))
    window = jnp.concatenate(earlier + [own_block], axis=0)
    window_keys = window[:, :, :head_dim]
    window_values = window[:, :, head_dim:]
    doc_ends = jnp.cumsum(lengths)
    key_pos = (shard - 3) * rows + jnp.arange(4 * rows, dtype=jnp.int32)
    visible = (key_pos[None, :] >= 0) & (key_pos[None, :] <= positions[:, None])
    visible = visible & (
        document_of(positions, doc_ends)[:, None] == document_of(key_pos, doc_ends)[None, :]
    )
    scale = 1.0 / math.sqrt(head_dim)
    scores = (
        jnp.einsum("tghd,kgd->ghtk", queries, window_keys, preferred_element_type=jnp.float32)
        * scale
    )
    scores = jnp.where(visible[None, None], scores, masked_score)
    peak = jnp.max(scores, axis=-1, keepdims=True)
    weights = jnp.exp(scores - peak)
    probs = (weights / jnp.sum(weights, axis=-1, keepdims=True)).astype(jnp.bfloat16)
    result = jnp.einsum("ghtk,kgd->tghd", probs, window_values, preferred_element_type=jnp.float32)
    return result.reshape(rows, 1, heads * head_dim).astype(jnp.bfloat16)


def solution(mesh):
    return jax.shard_map(
        per_device,
        mesh=mesh,
        in_specs=(P(("dp", "ctx"), None), P("dp"), P("ctx", "tp", None), P("ctx", "tp", None)),
        out_specs=P(("dp", "ctx"), "tp", None),
        check_vma=False,
    )
```

profile of v0, /device:TPU:2, one launch (start us, length us, event | category | flops | bytes accessed | tf_op | source)
XLA Modules:
  0.0 247.3 jit_solution(10694330591968272678)
XLA Ops:
  6.5 0.0 all-gather.3.cloned.1.call-start
  6.5 0.7 all-gather.3.cloned.1.call-update
  7.3 0.0 all-gather.5.cloned.1.call-start
  7.3 0.7 all-gather.5.cloned.1.call-update
  8.0 0.7 copy.17
  8.8 0.1 reduce-window.8
  8.9 0.1 reduce.2
  9.0 0.1 convert_reduce_fusion.1
  9.1 0.1 convert_reduce_fusion
  9.3 92.1 %all-gather.3.cloned.1.call-done = bf16[4096,1,256]{2,0,1:T(8,128)(2,1)} async-done(((bf16[128,1,256]{2,0,1:T(8,128)(2,1)}), bf16[4096,1,256]{2,0,1:T(8,128)(2,1)}) %all-gather.3.cloned.1.call-update) | async-done | bytes 2097168 | tf_op jit(solution)/shard_map/all_gather | solution.py:49
  101.3 4.2 %fusion.6 = f32[512,256]{0,1:T(8,128)S(1)} fusion(bf16[512,4096]{1,0:T(8,128)(2,1)} %param.4, bf16[4096,1,256]{2,0,1:T(8,128)(2,1)} %all-gather.3.cloned.1.call-done), kind=kOutput, calls=%fused_computation.10 | convolution fusion | flops 1073741824 | bytes 6815744 | tf_op jit(solution)/shard_map/dot_general | solution.py:44
  105.5 0.6 fusion.25
  106.2 4.7 %collective-permute-start.2 = (bf16[512,1,256]{0,2,1:T(8,128)(2,1)S(1)}, bf16[512,1,256]{0,2,1:T(8,128)(2,1)S(1)}, u32[]{:S(2)}, u32[]{:S(2)}) collective-permute-start(bf16[512,1,256]{0,2,1:T(8,128)(2,1)S(1)} %pad_maximum_fusion), channel_id=1, source_target_pairs={{0,8},{8,16},{16,24},{24,32},{32,40},{40,48},{48,56},{56,64},{64,7... | collective-permute-start | bytes 786440 | tf_op jit(solution)/shard_map/ppermute | solution.py:14
  110.8 3.7 %collective-permute-start.1 = (bf16[512,1,256]{0,2,1:T(8,128)(2,1)S(1)}, bf16[512,1,256]{0,2,1:T(8,128)(2,1)S(1)}, u32[]{:S(2)}, u32[]{:S(2)}) collective-permute-start(bf16[512,1,256]{0,2,1:T(8,128)(2,1)S(1)} %pad_maximum_fusion), channel_id=1, source_target_pairs={{0,16},{8,24},{16,32},{24,40},{32,48},{40,56},{48,64},{56,72},{64,... | collective-permute-start | bytes 786440 | tf_op jit(solution)/shard_map/ppermute | solution.py:14
  114.6 5.4 %collective-permute-start = (bf16[512,1,256]{0,2,1:T(8,128)(2,1)S(1)}, bf16[512,1,256]{0,2,1:T(8,128)(2,1)S(1)}, u32[]{:S(2)}, u32[]{:S(2)}) collective-permute-start(bf16[512,1,256]{0,2,1:T(8,128)(2,1)S(1)} %pad_maximum_fusion), channel_id=1, source_target_pairs={{0,24},{8,32},{16,40},{24,48},{32,56},{40,64},{48,72},{56,80},{64,... | collective-permute-start | bytes 786440 | tf_op jit(solution)/shard_map/ppermute | solution.py:14
  120.0 1.8 compare_and_fusion
  121.9 0.5 multiply_cosine_fusion
  122.4 2.3 collective-permute-done.2
  124.7 4.0 %collective-permute-done.1 = bf16[512,1,256]{0,2,1:T(8,128)(2,1)S(1)} collective-permute-done((bf16[512,1,256]{0,2,1:T(8,128)(2,1)S(1)}, bf16[512,1,256]{0,2,1:T(8,128)(2,1)S(1)}, u32[]{:S(2)}, u32[]{:S(2)}) %collective-permute-start.1) | collective-permute-done | bytes 262176 | tf_op jit(solution)/shard_map/ppermute | solution.py:14
  128.7 8.9 %collective-permute-done = bf16[512,1,256]{0,2,1:T(8,128)(2,1)S(1)} collective-permute-done((bf16[512,1,256]{0,2,1:T(8,128)(2,1)S(1)}, bf16[512,1,256]{0,2,1:T(8,128)(2,1)S(1)}, u32[]{:S(2)}, u32[]{:S(2)}) %collective-permute-start) | collective-permute-done | bytes 262176 | tf_op jit(solution)/shard_map/ppermute | solution.py:14
  137.6 0.1 maximum_maximum_fusion
  137.7 77.2 %all-gather.5.cloned.1.call-done = bf16[4096,1,512]{2,0,1:T(8,128)(2,1)} async-done(((bf16[128,1,512]{2,0,1:T(8,128)(2,1)}), bf16[4096,1,512]{2,0,1:T(8,128)(2,1)}) %all-gather.5.cloned.1.call-update) | async-done | bytes 4194320 | tf_op jit(solution)/shard_map/all_gather | solution.py:48
  214.9 6.5 %copy.18 = bf16[512,4096]{1,0:T(8,128)(2,1)} copy(bf16[512,4096]{0,1:T(8,128)(2,1)} %bitcast.63) | data formatting | bytes 8388608 | tf_op jit(solution)/shard_map/dot_general | solution.py:44
  221.3 5.8 %fusion.8 = f32[512,1,4,128]{0,3,2,1:T(8,128)S(1)} fusion(bf16[4,128,4096]{2,1,0:T(8,128)(2,1)} %bitcast.64, bf16[512,4096]{1,0:T(8,128)(2,1)} %param.4), kind=kOutput, calls=%fused_computation.12 | convolution fusion | flops 2147483648 | bytes 9437184 | tf_op jit(solution)/shard_map/dot_general | solution.py:44
  227.1 0.2 fusion.18
  227.3 3.2 %fusion.1 = (f32[4,512]{1,0:T(4,128)S(1)}, f32[2048,512,4]{1,0,2:T(8,128)S(1)}) fusion(pred[512,2048]{0,1:T(8,128)(4,1)S(1)} %compare_and_fusion, bf16[512,4,64]{0,2,1:T(8,128)(2,1)S(1)} %get-tuple-element.6, bf16[512,4,64]{0,2,1:T(8,128)(2,1)S(1)} %get-tuple-element.5, bf16[2048,1,256]{0,2,1:T(8,128)(2,1)S(1)} %maximum_maximum_fusion), kind=kOutput, calls=%fused_computation.4 | convolution fusion | flops 1087371264 | bytes 18882560 | tf_op jit(solution)/shard_map/tghd,kgd->ghtk/dot_general | solution.py:68
  230.5 3.7 %fusion = f32[4,512]{1,0:T(4,128)S(1)} fusion(f32[2048,512,4]{1,0,2:T(8,128)S(1)} %get-tuple-element.12, f32[4,512]{1,0:T(4,128)S(1)} %get-tuple-element.11, pred[512,2048]{0,1:T(8,128)(4,1)S(1)} %compare_and_fusion), kind=kLoop, calls=%fused_computation.3 | loop fusion | flops 16775168 | bytes 17842176 | tf_op jit(solution)/shard_map/reduce_sum | solution.py:74
  234.2 5.2 %fusion.11 = bf16[128,4,512]{2,0,1:T(8,128)(2,1)S(1)} fusion(f32[4,512]{1,0:T(4,128)S(1)} %fusion, f32[4,512]{1,0:T(4,128)S(1)} %get-tuple-element.11, f32[2048,512,4]{1,0,2:T(8,128)S(1)} %get-tuple-element.12, pred[512,2048]{0,1:T(8,128)(4,1)S(1)} %compare_and_fusion, bf16[2048,1,256]{0,2,1:T(8,128)(2,1)S(1)} %maximum_maximum_fusion), kind=kOutput, calls=%fused_computation.13 | convolution fusion | flops 1094975488 | bytes 18890752 | tf_op jit(solution)/shard_map/ghtk,kgd->tghd/dot_general | solution.py:75
  239.4 1.0 copy.22
  (9 shorter events, 0.1 us)
Async XLA Ops:
  6.5 94.8 %all-gather.3.cloned.1.call-start = ((), (), s32[]{:S(2)}) async-start(), calls=%async_computation | async-start | bytes 2162688 | tf_op jit(solution)/shard_map/all_gather | solution.py:49
  7.3 207.6 %all-gather.5.cloned.1.call-start = ((), (), s32[]{:S(2)}) async-start(), calls=%async_computation.1 | async-start | bytes 4325376 | tf_op jit(solution)/shard_map/all_gather | solution.py:48
  106.2 18.5 %collective-permute-start.2 = (bf16[512,1,256]{0,2,1:T(8,128)(2,1)S(1)}, bf16[512,1,256]{0,2,1:T(8,128)(2,1)S(1)}, u32[]{:S(2)}, u32[]{:S(2)}) collective-permute-start(bf16[512,1,256]{0,2,1:T(8,128)(2,1)S(1)} %pad_maximum_fusion), channel_id=1, source_target_pairs={{0,8},{8,16},{16,24},{24,32},{32,40},{40,48},{48,56},{56,64},{64,7... | collective-permute-start | bytes 786440 | tf_op jit(solution)/shard_map/ppermute | solution.py:14
  110.8 17.9 %collective-permute-start.1 = (bf16[512,1,256]{0,2,1:T(8,128)(2,1)S(1)}, bf16[512,1,256]{0,2,1:T(8,128)(2,1)S(1)}, u32[]{:S(2)}, u32[]{:S(2)}) collective-permute-start(bf16[512,1,256]{0,2,1:T(8,128)(2,1)S(1)} %pad_maximum_fusion), channel_id=1, source_target_pairs={{0,16},{8,24},{16,32},{24,40},{32,48},{40,56},{48,64},{56,72},{64,... | collective-permute-start | bytes 786440 | tf_op jit(solution)/shard_map/ppermute | solution.py:14
  114.6 23.0 %collective-permute-start = (bf16[512,1,256]{0,2,1:T(8,128)(2,1)S(1)}, bf16[512,1,256]{0,2,1:T(8,128)(2,1)S(1)}, u32[]{:S(2)}, u32[]{:S(2)}) collective-permute-start(bf16[512,1,256]{0,2,1:T(8,128)(2,1)S(1)} %pad_maximum_fusion), channel_id=1, source_target_pairs={{0,24},{8,32},{16,40},{24,48},{32,56},{40,64},{48,72},{56,80},{64,... | collective-permute-start | bytes 786440 | tf_op jit(solution)/shard_map/ppermute | solution.py:14
Sparse Core Ops, SparseCore 0:
  10.5 90.7 all-gather.2
  104.5 110.3 all-gather.4
where the time goes:
time: 248 us; the launch traced here: 247 us
  waiting for transfers between devices  186 us (75%)
  matrix products  18.4 us (7%)
  starting transfers between devices  13.9 us (6%)
  between operations  13.6 us (5%)
  local copies, waits for them, and re-layouts  8.24 us (3%)
  other arithmetic  7.4 us (3%)
    all_gather x1, waiting for transfers between devices, per_device(): kv_sum = project(lax.all_gather(kv_weight, 'ctx', axis=0, tiled=True))  92.1 us
    all_gather x1, waiting for transfers between devices, per_device(): q_sum = project(lax.all_gather(q_weight, 'ctx', axis=0, tiled=True))  77.2 us
    ppermute x3, waiting for transfers between devices, shifted(): lax.ppermute(value, axis, [(source, source + steps) for source in range(f...  15.2 us
    ppermute x3, starting transfers between devices, shifted(): lax.ppermute(value, axis, [(source, source + steps) for source in range(f...  13.8 us
    dot_general x2, matrix products, project(): jnp.dot(tokens, piece.reshape(piece.shape[0], -1), preferred_element_type...  9.98 us
    dot_general x1, local copies, waits for them, and re-layouts, project(): jnp.dot(tokens, piece.reshape(piece.shape[0], -1), preferred_element_type...  6.45 us
    dot_general x1, matrix products, per_device(): jnp.einsum('ghtk,kgd->tghd', probs, window_values, preferred_element_type...  5.18 us
  transfers between devices with their start and end apart: 5, of which 5 were waited for; matrix products, arithmetic and copies ran while one was open for 3% of the time, Pallas kernels for 0%

commit v1 on v0

v1 whole, which is shorter than its diff:
```python
import functools
import math

import jax
import jax.numpy as jnp
from jax import lax
from jax.experimental import pallas as pl
from jax.experimental.pallas import tpu as pltpu
from jax.sharding import Mesh
from jax.sharding import PartitionSpec as P

masked_score = -1e30
axes = ("dp", "z", "yh", "x", "yl")
z_size, yh_size, x_size, yl_size = (8, 4, 4, 2)
vmem_bytes = 48 * 1024 * 1024
tile = 128


def flat_device(dp, shard, column):
    return (dp * z_size * yh_size + shard) * (x_size * yl_size) + column


def shift_pairs(step):
    count = z_size * yh_size
    return [
        (flat_device(dp, shard, column), flat_device(dp, (shard + step(dp)) % count, column))
        for dp in range(2)
        for shard in range(count)
        for column in range(x_size * yl_size)
    ]


def ring_pairs(step):
    return shift_pairs(lambda dp: step(dp) * yh_size)


def swap_cores(value):
    return lax.ppermute(value, "dp", [(0, 1), (1, 0)])


def spread(value, axis, count):
    copies = jnp.broadcast_to(value[None], (count,) + value.shape)
    parts = lax.all_to_all(copies, axis, 0, 0)
    return parts.reshape(count * value.shape[0], value.shape[1])


def rotated(values, cosine, sine):
    return values * cosine + pltpu.roll(values, values.shape[-1] // 2, 1) * sine


def part_kernel(order, *refs, alone, both, carried):
    refs = list(refs)
    take = lambda count: [refs.pop(0) for _ in range(count)]
    mine, other = take(alone + both), take(both)
    weights = take(alone + both)
    totals = take(2) if carried else None
    out_mine, out_other = refs
    sums = [totals[0][...], totals[1][...]] if carried else [0.0, 0.0]
    for i, weight in enumerate(weights):
        sums[0] = sums[0] + jnp.dot(
            mine[i][...], weight[...], preferred_element_type=jnp.float32
        )
        if i >= alone:
            sums[1] = sums[1] + jnp.dot(
                other[i - alone][...], weight[...], preferred_element_type=jnp.float32
            )
    out_mine[...] = sums[0]
    out_other[...] = sums[1]


def project_part(order, mine, other, alone, both, totals, name):
    rows = mine.shape[0]
    steps = 2
    part = rows // steps
    weights = alone + both
    depth, columns = weights[0].shape
    tokens = lambda place: pl.BlockSpec((part, depth), lambda i, order: (i, order[place]))
    out = pl.BlockSpec((part, columns), lambda i, order: (i, 0))
    places = list(range(len(weights)))
    work = 2 * rows * depth * columns * (len(alone) + 2 * len(both))
    return pl.pallas_call(
        functools.partial(
            part_kernel, alone=len(alone), both=len(both), carried=bool(totals)
        ),
        grid_spec=pltpu.PrefetchScalarGridSpec(
            num_scalar_prefetch=1,
            grid=(steps,),
            in_specs=[tokens(place) for place in places + places[len(alone) :]]
            + [pl.BlockSpec((depth, columns), lambda i, order: (0, 0))] * len(weights)
            + [out] * len(totals),
            out_specs=[out, out],
        ),
        out_shape=[jax.ShapeDtypeStruct((rows, columns), jnp.float32)] * 2,
        compiler_params=pltpu.CompilerParams(vmem_limit_bytes=vmem_bytes),
        cost_estimate=pl.CostEstimate(
            flops=work, bytes_accessed=work // 256, transcendentals=0
        ),
        name=name,
    )(order, *[mine] * len(weights), *[other] * len(both), *weights, *totals)


def finish_kernel(
    scalars, mine, other, weight, total_mine, total_other, cosine, sine, out_mine, out_other, *, part
):
    head_dim = cosine.shape[1]
    for source, total, out in ((mine, total_mine, out_mine), (other, total_other, out_other)):
        value = total[...] + jnp.dot(
            source[...], weight[...], preferred_element_type=jnp.float32
        )
        for head in range(out.shape[1] // head_dim):
            columns = slice(head * head_dim, (head + 1) * head_dim)
            turned = rotated(value[:, columns], cosine[...], sine[...])
            if part == "kv":
                turned = jnp.where(scalars[1] == 0, turned, value[:, columns])
            out[:, columns] = turned.astype(out.dtype)


def finish(scalars, mine, other, weight, totals, cosine, sine, columns, place, part):
    rows, depth = mine.shape[0], weight.shape[0]
    head_dim = cosine.shape[1]
    tokens = pl.BlockSpec((rows, depth), lambda i, scalars: (0, scalars[0]))
    total = pl.BlockSpec((rows, columns), lambda i, scalars: (0, place))
    table = pl.BlockSpec((rows, head_dim), lambda i, scalars: (0, 0))
    out = pl.BlockSpec((rows, columns), lambda i, scalars: (0, 0))
    return pl.pallas_call(
        functools.partial(finish_kernel, part=part),
        grid_spec=pltpu.PrefetchScalarGridSpec(
            num_scalar_prefetch=1,
            grid=(1,),
            in_specs=[
                tokens,
                tokens,
                pl.BlockSpec((depth, columns), lambda i, scalars: (0, place)),
                total,
                total,
                table,
                table,
            ],
            out_specs=[out, out],
        ),
        out_shape=[jax.ShapeDtypeStruct((rows, columns), jnp.bfloat16)] * 2,
        compiler_params=pltpu.CompilerParams(vmem_limit_bytes=vmem_bytes),
        cost_estimate=pl.CostEstimate(
            flops=4 * rows * depth * columns,
            bytes_accessed=4 * rows * depth + 8 * rows * columns,
            transcendentals=0,
        ),
        name=part + "_finish",
    )(scalars, mine, other, weight, *totals, cosine, sine)


def score_pieces(queries, start, pieces, first):
    head_dim = queries.shape[1]
    scale = math.log2(math.e) / math.sqrt(head_dim)
    contract = (((1,), (1,)), ((), ()))
    scores = []
    for block, low, high, place in pieces:
        part = lax.dot_general(
            queries, block[low:high, :head_dim], contract, preferred_element_type=jnp.float32
        )
        column = place + low + lax.broadcasted_iota(jnp.int32, part.shape, 1)
        seen = column >= start
        if high <= first + tile and place == 3 * block.shape[0]:
            row = lax.broadcasted_iota(jnp.int32, part.shape, 0) % tile
            seen = seen & (column <= row + (place + first))
        scores.append(jnp.where(seen, part * scale, masked_score))
    return scores


def gather_pieces(scores, pieces, peak):
    total, result = 0.0, 0.0
    for part, (block, low, high, place) in zip(scores, pieces):
        head_dim = block.shape[1] // 2
        weights = jnp.exp2(part - peak)
        total = total + jnp.sum(weights, axis=1, keepdims=True)
        result = result + jnp.dot(
            weights.astype(jnp.bfloat16),
            block[low:high, head_dim:],
            preferred_element_type=jnp.float32,
        )
    return total, result


def tile_inputs(half, q_mine, q_other, starts, first, head_dim):
    here = slice(first, first + tile)
    queries = jnp.where(half == 0, q_mine[here], q_other[here])
    heads = queries.shape[1] // head_dim
    queries = jnp.concatenate(
        [queries[:, h * head_dim : (h + 1) * head_dim] for h in range(heads)], axis=0
    )
    return queries, jnp.concatenate([starts[here]] * heads, axis=0)


def near_kernel(core, q_mine, q_other, one_three, three_one, own, starts, partial, stats, three, one):
    half = pl.program_id(0)

    @pl.when((half == 0) & (core[0] == 0))
    def _():
        one[...] = one_three[...]
        three[...] = three_one[...]

    @pl.when((half == 0) & (core[0] == 1))
    def _():
        three[...] = one_three[...]
        one[...] = three_one[...]

    rows, head_dim = own.shape[0], own.shape[1] // 2
    for first in range(0, rows, tile):
        queries, start = tile_inputs(half, q_mine, q_other, starts, first, head_dim)
        pieces = [
            (three, first, rows, 0),
            (one, 0, rows, 2 * rows),
            (own, 0, first + tile, 3 * rows),
        ]
        scores = score_pieces(queries, start, pieces, first)
        peak = functools.reduce(
            jnp.maximum, [jnp.max(part, axis=1, keepdims=True) for part in scores]
        )
        total, result = gather_pieces(scores, pieces, peak)
        height = queries.shape[0]
        place = slice(first // tile * height, (first // tile + 1) * height)
        partial[place] = result
        lane = lax.broadcasted_iota(jnp.int32, (height, head_dim), 1)
        stats[place] = jnp.where(lane < head_dim // 2, peak, total)


def last_kernel(core, q_mine, q_other, two, starts, partial, stats, out):
    half = pl.program_id(0)
    rows, head_dim = two.shape[0], two.shape[1] // 2
    for first in range(0, rows, tile):
        queries, start = tile_inputs(half, q_mine, q_other, starts, first, head_dim)
        height = queries.shape[0]
        pieces = [(two, 0, rows, rows)]
        scores = score_pieces(queries, start, pieces, first)
        place = slice(first // tile * height, (first // tile + 1) * height)
        peak = stats[place, 0:1]
        total = stats[place, head_dim // 2 : head_dim // 2 + 1]
        top = jnp.maximum(peak, jnp.max(scores[0], axis=1, keepdims=True))
        more, result = gather_pieces(scores, pieces, top)
        keep = jnp.exp2(peak - top)
        result = ((partial[place] * keep + result) / (total * keep + more)).astype(out.dtype)
        for h in range(height // tile):
            out[first : first + tile, h * head_dim : (h + 1) * head_dim] = result[
                h * tile : (h + 1) * tile
            ]


def attend(core, q_mine, q_other, one_three, three_one, two, own, starts):
    rows, columns = q_mine.shape
    head_dim = own.shape[1] // 2
    height = rows * columns // head_dim
    whole = lambda array: pl.BlockSpec(array.shape, lambda i, core: (0, 0))
    args = (q_mine, q_other, one_three, three_one, own, starts)
    kept = pl.BlockSpec((height, head_dim), lambda i, core: (i, 0))
    partial, stats = pl.pallas_call(
        near_kernel,
        grid_spec=pltpu.PrefetchScalarGridSpec(
            num_scalar_prefetch=1,
            grid=(2,),
            in_specs=[whole(array) for array in args],
            out_specs=[kept, kept],
            scratch_shapes=[pltpu.VMEM(own.shape, own.dtype)] * 2,
        ),
        out_shape=[jax.ShapeDtypeStruct((2 * height, head_dim), jnp.float32)] * 2,
        compiler_params=pltpu.CompilerParams(vmem_limit_bytes=vmem_bytes),
        cost_estimate=pl.CostEstimate(
            flops=8 * rows * 9 * tile * columns,
            bytes_accessed=16 * rows * columns,
            transcendentals=4 * rows * 9 * tile,
        ),
        name="attend_near",
    )(core, *args)
    args = (q_mine, q_other, two, starts)
    return pl.pallas_call(
        last_kernel,
        grid_spec=pltpu.PrefetchScalarGridSpec(
            num_scalar_prefetch=1,
            grid=(2,),
            in_specs=[whole(array) for array in args] + [kept, kept],
            out_specs=pl.BlockSpec((rows, columns), lambda i, core: (0, (i + core[0]) % 2)),
        ),
        out_shape=jax.ShapeDtypeStruct((rows, 2 * columns), jnp.bfloat16),
        compiler_params=pltpu.CompilerParams(vmem_limit_bytes=vmem_bytes),
        cost_estimate=pl.CostEstimate(
            flops=8 * rows * 4 * tile * columns,
            bytes_accessed=16 * rows * columns,
            transcendentals=4 * rows * 4 * tile,
        ),
        name="attend_last",
    )(core, *args, partial, stats)


def per_device(tokens, lengths, q_weight, kv_weight):
    rows, features = tokens.shape
    head_dim = kv_weight.shape[2] // 2
    core = lax.axis_index("dp")
    plane = lax.axis_index("z")
    shard = plane * yh_size + lax.axis_index("yh")

    depth = q_weight.shape[0]
    half_cols = q_weight.shape[2] // 2
    columns = half_cols + head_dim
    q_half = lax.dynamic_slice_in_dim(q_weight[:, 0], core * half_cols, half_cols, 1)
    kv_half = lax.dynamic_slice_in_dim(kv_weight[:, 0], core * head_dim, head_dim, 1)
    mine = jnp.concatenate([q_half, kv_half], axis=1)
    block = spread(mine, "yh", yh_size)

    positions = shard * rows + jnp.arange(rows, dtype=jnp.int32)
    half = head_dim // 2
    freqs = jnp.exp(
        jnp.arange(half, dtype=jnp.float32) * (-2.0 * math.log(500000.0) / head_dim)
    )
    angle = positions.astype(jnp.float32)[:, None] * freqs[None, :]
    cosine = jnp.concatenate([jnp.cos(angle)] * 2, axis=1)
    sine = jnp.sin(angle)
    sine = jnp.concatenate([-sine, sine], axis=1)
    docs = jnp.arange(lengths.shape[0])
    ends = jnp.sum(jnp.where(docs[None, :] <= docs[:, None], lengths[None, :], 0), axis=1)
    starts = jnp.max(jnp.where(ends[None, :] <= positions[:, None], ends[None, :], 0), axis=1)
    starts = (starts - (shard - 3) * rows)[:, None]

    block, cosine, sine, starts, tokens = lax.optimization_barrier(
        (block, cosine, sine, starts, tokens)
    )
    tokens_other = swap_cores(tokens)
    ahead, back = ring_pairs(lambda dp: 1 - 2 * dp), ring_pairs(lambda dp: 2 * dp - 1)
    aheads, backs = [block], [block]
    for _ in range(z_size // 2 - 1):
        aheads.append(lax.ppermute(aheads[-1], axes, ahead))
        backs.append(lax.ppermute(backs[-1], axes, back))
    far = lax.ppermute(aheads[-1], axes, ahead)
    blocks = [block] + [part for pair in zip(aheads[1:], backs[1:]) for part in pair]
    steps = jnp.array([0, -1, 1, -2, 2, -3, 3, 4], jnp.int32)
    order = (plane + steps * (1 - 2 * core)) % z_size
    totals = project_part(order[:5], tokens, tokens_other, [], blocks[:5], [], "near")
    totals = project_part(
        order[5:7], tokens, tokens_other, [], blocks[5:], list(totals), "farther"
    )

    scalars = jnp.stack([order[-1], core])
    last = (scalars, tokens, tokens_other, far, totals, cosine, sine)
    kv_mine, kv_theirs = finish(*last, head_dim, half_cols // head_dim, "kv")
    kv_other = swap_cores(kv_theirs)
    first = core == 0
    own = jnp.concatenate(
        [lax.select(first, kv_mine, kv_other), lax.select(first, kv_other, kv_mine)], axis=1
    )
    one_three = lax.ppermute(own, axes, shift_pairs(lambda dp: 1 + 2 * dp))
    three_one = lax.ppermute(own, axes, shift_pairs(lambda dp: 3 - 2 * dp))
    two = lax.ppermute(one_three, axes, shift_pairs(lambda dp: 1 - 2 * dp))
    core_index = core.reshape(1).astype(jnp.int32)
    q_mine, q_theirs = finish(*last, half_cols, 0, "q")
    q_other = swap_cores(q_theirs)
    out = attend(core_index, q_mine, q_other, one_three, three_one, two, own, starts)
    return out[:, None]


def solution(mesh):
    split = Mesh(mesh.devices.reshape(2, z_size, yh_size, x_size, yl_size), axes)
    column = P(("z", "yh"), ("x", "yl"), None)
    return jax.shard_map(
        per_device,
        mesh=split,
        in_specs=(P(("dp", "z", "yh"), None), P("dp"), column, column),
        out_specs=P(("dp", "z", "yh"), ("x", "yl"), None),
        check_vma=False,
    )
```

time: 248 us -> 127 us (0.51)
  the two profiles are of different devices: /device:TPU:2 before, /device:TPU:196 now
where the time goes in v1:
time: 127 us
  starting transfers between devices  50.2 us (40%)
  waiting for transfers between devices  45.9 us (36%)
  Pallas kernels  23.3 us (18%)
  other arithmetic  3.6 us (3%)
  local copies, waits for them, and re-layouts  3.25 us (3%)
    ppermute x3, waiting for transfers between devices, per_device(): aheads.append(lax.ppermute(aheads[-1], axes, ahead))  20 us
    ppermute x3, starting transfers between devices, per_device(): aheads.append(lax.ppermute(aheads[-1], axes, ahead))  16.7 us
    ppermute x1, waiting for transfers between devices, per_device(): three_one = lax.ppermute(own, axes, shift_pairs(lambda dp: 3 - 2 * dp))  11.8 us
    all_to_all x1, waiting for transfers between devices, spread(): parts = lax.all_to_all(copies, axis, 0, 0)  10.6 us
    pallas_call x2, Pallas kernels, project_part(): pl.pallas_call(functools.partial(part_kernel, alone=len(alone), both=len(...  8.81 us
    all_to_all x1, starting transfers between devices, spread(): parts = lax.all_to_all(copies, axis, 0, 0)  7.09 us
    ppermute x3, starting transfers between devices, per_device(): backs.append(lax.ppermute(backs[-1], axes, back))  5.76 us
    ppermute x3, starting transfers between devices, swap_cores(): return lax.ppermute(value, 'dp', [(0, 1), (1, 0)])  5.74 us
  transfers between devices with their start and end apart: 14, of which 7 were waited for; matrix products, arithmetic and copies ran while one was open for 3% of the time, Pallas kernels for 13%

profile of v1, /device:TPU:196, one launch (start us, length us, event | category | flops | bytes accessed | tf_op | source)
XLA Modules:
  0.0 126.6 jit_solution(14269358517463294668)
XLA Ops:
  0.0 0.0 copy-start
  0.0 0.9 copy-done
  0.9 0.8 dynamic-slice_bitcast_fusion.1
  1.7 0.8 broadcast_in_dim.22
  2.5 7.1 %all-to-all-start = ((bf16[4,128,384]{2,1,0:T(8,128)(2,1)}), bf16[4,128,384]{2,1,0:T(8,128)(2,1)S(1)}, u32[]{:S(2)}, u32[]{:S(2)}) async-start(bf16[4,128,384]{2,1,0:T(8,128)(2,1)} %broadcast_in_dim.22), calls=%async_computation | async-start | bytes 786432 | tf_op jit(solution)/shard_map/all_to_all | solution.py:43
  9.6 1.0 fusion
  10.6 0.8 select_reduce_fusion.1
  11.4 0.1 select_reduce_fusion
  11.5 0.1 pad_maximum_fusion.cosine
  11.6 0.1 pad_maximum_fusion.1.sine
  11.8 10.6 %all-to-all-done = bf16[4,128,384]{2,1,0:T(8,128)(2,1)S(1)} async-done(((bf16[4,128,384]{2,1,0:T(8,128)(2,1)}), bf16[4,128,384]{2,1,0:T(8,128)(2,1)S(1)}, u32[]{:S(2)}, u32[]{:S(2)}) %all-to-all-start) | async-done | bytes 393248 | tf_op jit(solution)/shard_map/all_to_all | solution.py:43
  22.4 1.9 %collective-permute-start = (bf16[512,4096]{1,0:T(8,128)(2,1)}, bf16[512,4096]{1,0:T(8,128)(2,1)}, u32[]{:S(2)}, u32[]{:S(2)}) collective-permute-start(bf16[512,4096]{1,0:T(8,128)(2,1)} %mine.1), channel_id=1, source_target_pairs={{0,256},{256,0},{1,257},{257,1},{2,258},{258,2},{3,259},{259,3},{4... | collective-permute-start | bytes 12582920 | tf_op jit(solution)/shard_map/ppermute | solution.py:38
  24.3 5.5 %collective-permute-start.1 = (bf16[512,384]{1,0:T(8,128)(2,1)S(1)}, bf16[512,384]{1,0:T(8,128)(2,1)S(1)}, u32[]{:S(2)}, u32[]{:S(2)}) collective-permute-start(bf16[512,384]{1,0:T(8,128)(2,1)S(1)} %bitcast.9), channel_id=1, source_target_pairs={{0,32},{1,33},{2,34},{3,35},{4,36},{5,37},{6,38},{7,39},{8,40},{9,... | collective-permute-start | bytes 1179656 | tf_op jit(solution)/shard_map/ppermute | solution.py:329
  29.8 1.9 %collective-permute-start.5 = (bf16[512,384]{1,0:T(8,128)(2,1)S(1)}, bf16[512,384]{1,0:T(8,128)(2,1)S(1)}, u32[]{:S(2)}, u32[]{:S(2)}) collective-permute-start(bf16[512,384]{1,0:T(8,128)(2,1)S(1)} %bitcast.10), channel_id=1, source_target_pairs={{0,224},{1,225},{2,226},{3,227},{4,228},{5,229},{6,230},{7,231},{8... | collective-permute-start | bytes 1179656 | tf_op jit(solution)/shard_map/ppermute | solution.py:330
  31.7 6.0 %collective-permute-done.1.refs_11_ = bf16[512,384]{1,0:T(8,128)(2,1)S(1)} collective-permute-done((bf16[512,384]{1,0:T(8,128)(2,1)S(1)}, bf16[512,384]{1,0:T(8,128)(2,1)S(1)}, u32[]{:S(2)}, u32[]{:S(2)}) %collective-permute-start.1) | collective-permute-done | bytes 393248 | tf_op jit(solution)/shard_map/ppermute | solution.py:329
  37.7 5.6 %collective-permute-start.2 = (bf16[512,384]{1,0:T(8,128)(2,1)S(1)}, bf16[512,384]{1,0:T(8,128)(2,1)S(1)}, u32[]{:S(2)}, u32[]{:S(2)}) collective-permute-start(bf16[512,384]{1,0:T(8,128)(2,1)S(1)} %collective-permute-done.1.refs_11_), channel_id=1, source_target_pairs={{0,32},{1,33},{2,34},{3,35},{4,36},{5,37},{6,38},{7,39},{8,40},{9,... | collective-permute-start | bytes 1179656 | tf_op jit(solution)/shard_map/ppermute | solution.py:329
  43.3 0.0 collective-permute-done.5.refs_12_
  43.4 1.9 %collective-permute-start.6 = (bf16[512,384]{1,0:T(8,128)(2,1)S(1)}, bf16[512,384]{1,0:T(8,128)(2,1)S(1)}, u32[]{:S(2)}, u32[]{:S(2)}) collective-permute-start(bf16[512,384]{1,0:T(8,128)(2,1)S(1)} %collective-permute-done.5.refs_12_), channel_id=1, source_target_pairs={{0,224},{1,225},{2,226},{3,227},{4,228},{5,229},{6,230},{7,231},{8... | collective-permute-start | bytes 1179656 | tf_op jit(solution)/shard_map/ppermute | solution.py:330
  45.3 7.3 %collective-permute-done.2.refs_13_ = bf16[512,384]{1,0:T(8,128)(2,1)S(1)} collective-permute-done((bf16[512,384]{1,0:T(8,128)(2,1)S(1)}, bf16[512,384]{1,0:T(8,128)(2,1)S(1)}, u32[]{:S(2)}, u32[]{:S(2)}) %collective-permute-start.2) | collective-permute-done | bytes 393248 | tf_op jit(solution)/shard_map/ppermute | solution.py:329
  52.5 5.6 %collective-permute-start.3 = (bf16[512,384]{1,0:T(8,128)(2,1)S(1)}, bf16[512,384]{1,0:T(8,128)(2,1)S(1)}, u32[]{:S(2)}, u32[]{:S(2)}) collective-permute-start(bf16[512,384]{1,0:T(8,128)(2,1)S(1)} %collective-permute-done.2.refs_13_), channel_id=1, source_target_pairs={{0,32},{1,33},{2,34},{3,35},{4,36},{5,37},{6,38},{7,39},{8,40},{9,... | collective-permute-start | bytes 1179656 | tf_op jit(solution)/shard_map/ppermute | solution.py:329
  58.1 0.0 collective-permute-done.6.refs_14_
  58.2 1.9 %collective-permute-start.7 = (bf16[512,384]{1,0:T(8,128)(2,1)S(1)}, bf16[512,384]{1,0:T(8,128)(2,1)S(1)}, u32[]{:S(2)}, u32[]{:S(2)}) collective-permute-start(bf16[512,384]{1,0:T(8,128)(2,1)S(1)} %collective-permute-done.6.refs_14_), channel_id=1, source_target_pairs={{0,224},{1,225},{2,226},{3,227},{4,228},{5,229},{6,230},{7,231},{8... | collective-permute-start | bytes 1179656 | tf_op jit(solution)/shard_map/ppermute | solution.py:330
  60.1 6.7 %collective-permute-done.3.refs_4_ = bf16[512,384]{1,0:T(8,128)(2,1)S(1)} collective-permute-done((bf16[512,384]{1,0:T(8,128)(2,1)S(1)}, bf16[512,384]{1,0:T(8,128)(2,1)S(1)}, u32[]{:S(2)}, u32[]{:S(2)}) %collective-permute-start.3) | collective-permute-done | bytes 393248 | tf_op jit(solution)/shard_map/ppermute | solution.py:329
  66.8 5.6 %collective-permute-start.4 = (bf16[512,384]{1,0:T(8,128)(2,1)S(1)}, bf16[512,384]{1,0:T(8,128)(2,1)S(1)}, u32[]{:S(2)}, u32[]{:S(2)}) collective-permute-start(bf16[512,384]{1,0:T(8,128)(2,1)S(1)} %collective-permute-done.3.refs_4_), channel_id=1, source_target_pairs={{0,32},{1,33},{2,34},{3,35},{4,36},{5,37},{6,38},{7,39},{8,40},{9,... | collective-permute-start | bytes 1179656 | tf_op jit(solution)/shard_map/ppermute | solution.py:331
  72.4 0.7 and_select_fusion
  73.0 0.1 slice.10.order
  73.1 0.6 slice.9
  73.7 0.7 pad_add_fusion.scalars
  74.4 0.0 collective-permute-done.refs_5_.refs_6_.refs_7_.refs_8_.refs_9_.refs_2_.refs_3_.other
  74.4 5.5 %near.1 = (f32[512,384]{1,0:T(8,128)S(1)}, f32[512,384]{1,0:T(8,128)S(1)}) custom-call(s32[5]{0:T(128)S(1)} %bitcast.12, bf16[512,4096]{1,0:T(8,128)(2,1)} %mine.1, bf16[512,4096]{1,0:T(8,128)(2,1)} %mine.1, bf16[512,4096]{1,0:T(8,128)(2,1)} %mine.1, bf16[512,4096]{1,0:T(8,128)(2,1)} %mine.1, bf16[512,4096]{1,0:T(8,128)(2,1)} %mine.1, ...), custom_call_target="tpu_custom_call" | custom-call | flops 2013265920 | bytes 7864320 | tf_op jit(solution)/shard_map/near/pallas_call | solution.py:81
  80.0 0.0 collective-permute-done.7.refs_5_
  80.0 3.3 %farther.1 = (f32[512,384]{1,0:T(8,128)S(1)}, f32[512,384]{1,0:T(8,128)S(1)}) custom-call(s32[2]{0:T(128)S(1)} %slice.10.order, bf16[512,4096]{1,0:T(8,128)(2,1)} %mine.1, bf16[512,4096]{1,0:T(8,128)(2,1)} %mine.1, bf16[512,4096]{1,0:T(8,128)(2,1)} %collective-permute-done.refs_5_.refs_6_.refs_7_.refs_8_.refs_9_.refs_2_.refs_3_.other, ...), custom_call_target="tpu_custom_call" | custom-call | flops 805306368 | bytes 3145728 | tf_op jit(solution)/shard_map/farther/pallas_call | solution.py:81
  83.3 0.0 collective-permute-done.4.weight
  83.3 2.3 %kv_finish.1 = (bf16[512,128]{1,0:T(8,128)(2,1)S(1)}, bf16[512,128]{1,0:T(8,128)(2,1)S(1)}) custom-call(s32[2]{0:T(128)S(1)} %pad_add_fusion.scalars, bf16[512,4096]{1,0:T(8,128)(2,1)} %mine.1, bf16[512,4096]{1,0:T(8,128)(2,1)} %collective-permute-done.refs_5_.refs_6_.refs_7_.refs_8_.refs_9_.refs_2_.refs_3_.other, ...), custom_call_target="tpu_custom_call" | custom-call | flops 134217728 | bytes 1572864 | tf_op jit(solution)/shard_map/kv_finish/pallas_call | solution.py:125
  85.5 1.9 %collective-permute-start.9 = (bf16[512,128]{1,0:T(8,128)(2,1)S(1)}, bf16[512,128]{1,0:T(8,128)(2,1)S(1)}, u32[]{:S(2)}, u32[]{:S(2)}) collective-permute-start(bf16[512,128]{1,0:T(8,128)(2,1)S(1)} %get-tuple-element.31), channel_id=1, source_target_pairs={{0,256},{256,0},{1,257},{257,1},{2,258},{258,2},{3,259},{259,3},{4... | collective-permute-start | bytes 393224 | tf_op jit(solution)/shard_map/ppermute | solution.py:38
  87.5 1.3 %collective-permute-done.9 = bf16[512,128]{1,0:T(8,128)(2,1)S(1)} collective-permute-done((bf16[512,128]{1,0:T(8,128)(2,1)S(1)}, bf16[512,128]{1,0:T(8,128)(2,1)S(1)}, u32[]{:S(2)}, u32[]{:S(2)}) %collective-permute-start.9) | collective-permute-done | bytes 131104 | tf_op jit(solution)/shard_map/ppermute | solution.py:38
  88.8 4.4 %collective-permute-start.10 = (bf16[512,256]{1,0:T(8,128)(2,1)S(1)}, bf16[512,256]{1,0:T(8,128)(2,1)S(1)}, u32[]{:S(2)}, u32[]{:S(2)}) collective-permute-start(bf16[512,256]{1,0:T(8,128)(2,1)S(1)} %pad_maximum_fusion.2.own), channel_id=1, source_target_pairs={{0,8},{1,9},{2,10},{3,11},{4,12},{5,13},{6,14},{7,15},{8,16},{9,17... | collective-permute-start | bytes 786440 | tf_op jit(solution)/shard_map/ppermute | solution.py:348
  93.2 3.1 %q_finish.1 = (bf16[512,256]{1,0:T(8,128)(2,1)S(1)}, bf16[512,256]{1,0:T(8,128)(2,1)}) custom-call(s32[2]{0:T(128)S(1)} %pad_add_fusion.scalars, bf16[512,4096]{1,0:T(8,128)(2,1)} %mine.1, bf16[512,4096]{1,0:T(8,128)(2,1)} %collective-permute-done.refs_5_.refs_6_.refs_7_.refs_8_.refs_9_.refs_2_.refs_3_.other, ...), custom_call_target="tpu_custom_call" | custom-call | flops 268435456 | bytes 2097152 | tf_op jit(solution)/shard_map/q_finish/pallas_call | solution.py:125
  96.3 1.9 %collective-permute-start.8 = (bf16[512,256]{1,0:T(8,128)(2,1)}, bf16[512,256]{1,0:T(8,128)(2,1)S(1)}, u32[]{:S(2)}, u32[]{:S(2)}) collective-permute-start(bf16[512,256]{1,0:T(8,128)(2,1)} %get-tuple-element.29), channel_id=1, source_target_pairs={{0,256},{256,0},{1,257},{257,1},{2,258},{258,2},{3,259},{259,3},{4... | collective-permute-start | bytes 786440 | tf_op jit(solution)/shard_map/ppermute | solution.py:38
  98.2 3.0 %collective-permute-start.12 = (bf16[512,256]{1,0:T(8,128)(2,1)S(1)}, bf16[512,256]{1,0:T(8,128)(2,1)S(1)}, u32[]{:S(2)}, u32[]{:S(2)}) collective-permute-start(bf16[512,256]{1,0:T(8,128)(2,1)S(1)} %pad_maximum_fusion.2.own), channel_id=1, source_target_pairs={{0,24},{1,25},{2,26},{3,27},{4,28},{5,29},{6,30},{7,31},{8,32},{9,... | collective-permute-start | bytes 786440 | tf_op jit(solution)/shard_map/ppermute | solution.py:349
  101.3 2.2 %collective-permute-done.10.one_three = bf16[512,256]{1,0:T(8,128)(2,1)S(1)} collective-permute-done((bf16[512,256]{1,0:T(8,128)(2,1)S(1)}, bf16[512,256]{1,0:T(8,128)(2,1)S(1)}, u32[]{:S(2)}, u32[]{:S(2)}) %collective-permute-start.10) | collective-permute-done | bytes 262176 | tf_op jit(solution)/shard_map/ppermute | solution.py:348
  103.5 1.9 %collective-permute-start.11 = (bf16[512,256]{1,0:T(8,128)(2,1)S(1)}, bf16[512,256]{1,0:T(8,128)(2,1)S(1)}, u32[]{:S(2)}, u32[]{:S(2)}) collective-permute-start(bf16[512,256]{1,0:T(8,128)(2,1)S(1)} %collective-permute-done.10.one_three), channel_id=1, source_target_pairs={{0,8},{1,9},{2,10},{3,11},{4,12},{5,13},{6,14},{7,15},{8,16},{9,17... | collective-permute-start | bytes 786440 | tf_op jit(solution)/shard_map/ppermute | solution.py:350
  105.4 0.1 copy.9.starts
  105.5 0.0 collective-permute-done.8.q_other
  105.5 11.8 %collective-permute-done.12.three_one = bf16[512,256]{1,0:T(8,128)(2,1)S(1)} collective-permute-done((bf16[512,256]{1,0:T(8,128)(2,1)S(1)}, bf16[512,256]{1,0:T(8,128)(2,1)S(1)}, u32[]{:S(2)}, u32[]{:S(2)}) %collective-permute-start.12) | collective-permute-done | bytes 262176 | tf_op jit(solution)/shard_map/ppermute | solution.py:349
  117.4 4.8 %attend_near.1 = (f32[2048,128]{1,0:T(8,128)S(1)}, f32[2048,128]{1,0:T(8,128)S(1)}) custom-call(s32[1]{0:T(128)} %bitcast.core, bf16[512,256]{1,0:T(8,128)(2,1)S(1)} %get-tuple-element.28.q_mine, bf16[512,256]{1,0:T(8,128)(2,1)S(1)} %collective-permute-done.8.q_other, bf16[512,256]{1,0:T(8,128)(2,1)S(1)} %collective-permute-done.10.one_three, ...), custom_call_target="tpu_custom_call" | custom-call | flops 1207959552 | bytes 2097152 | tf_op jit(solution)/shard_map/attend_near/pallas_call | solution.py:255
  122.1 0.0 collective-permute-done.11.two
  122.1 4.4 %attend_last.1 = bf16[512,512]{1,0:T(8,128)(2,1)} custom-call(s32[1]{0:T(128)} %bitcast.core, bf16[512,256]{1,0:T(8,128)(2,1)S(1)} %get-tuple-element.28.q_mine, bf16[512,256]{1,0:T(8,128)(2,1)S(1)} %collective-permute-done.8.q_other, bf16[512,256]{1,0:T(8,128)(2,1)S(1)} %collective-permute-done.11.two, s32[512,1]{1,0:T(8,128)S(1)} %copy.9.starts, ...), custom_call_target="tpu_custom_call" | custom-call | flops 536870912 | bytes 2097152 | tf_op jit(solution)/shard_map/attend_last/pallas_call | solution.py:274
  (7 shorter events, 0.1 us)
Async XLA Ops:
  0.0 0.9 copy-start
  2.5 19.9 %all-to-all-start = ((bf16[4,128,384]{2,1,0:T(8,128)(2,1)}), bf16[4,128,384]{2,1,0:T(8,128)(2,1)S(1)}, u32[]{:S(2)}, u32[]{:S(2)}) async-start(bf16[4,128,384]{2,1,0:T(8,128)(2,1)} %broadcast_in_dim.22), calls=%async_computation | async-start | bytes 786432 | tf_op jit(solution)/shard_map/all_to_all | solution.py:43
  22.4 52.1 %collective-permute-start = (bf16[512,4096]{1,0:T(8,128)(2,1)}, bf16[512,4096]{1,0:T(8,128)(2,1)}, u32[]{:S(2)}, u32[]{:S(2)}) collective-permute-start(bf16[512,4096]{1,0:T(8,128)(2,1)} %mine.1), channel_id=1, source_target_pairs={{0,256},{256,0},{1,257},{257,1},{2,258},{258,2},{3,259},{259,3},{4... | collective-permute-start | bytes 12582920 | tf_op jit(solution)/shard_map/ppermute | solution.py:38
  24.3 13.5 %collective-permute-start.1 = (bf16[512,384]{1,0:T(8,128)(2,1)S(1)}, bf16[512,384]{1,0:T(8,128)(2,1)S(1)}, u32[]{:S(2)}, u32[]{:S(2)}) collective-permute-start(bf16[512,384]{1,0:T(8,128)(2,1)S(1)} %bitcast.9), channel_id=1, source_target_pairs={{0,32},{1,33},{2,34},{3,35},{4,36},{5,37},{6,38},{7,39},{8,40},{9,... | collective-permute-start | bytes 1179656 | tf_op jit(solution)/shard_map/ppermute | solution.py:329
  29.8 13.6 %collective-permute-start.5 = (bf16[512,384]{1,0:T(8,128)(2,1)S(1)}, bf16[512,384]{1,0:T(8,128)(2,1)S(1)}, u32[]{:S(2)}, u32[]{:S(2)}) collective-permute-start(bf16[512,384]{1,0:T(8,128)(2,1)S(1)} %bitcast.10), channel_id=1, source_target_pairs={{0,224},{1,225},{2,226},{3,227},{4,228},{5,229},{6,230},{7,231},{8... | collective-permute-start | bytes 1179656 | tf_op jit(solution)/shard_map/ppermute | solution.py:330
  37.7 14.8 %collective-permute-start.2 = (bf16[512,384]{1,0:T(8,128)(2,1)S(1)}, bf16[512,384]{1,0:T(8,128)(2,1)S(1)}, u32[]{:S(2)}, u32[]{:S(2)}) collective-permute-start(bf16[512,384]{1,0:T(8,128)(2,1)S(1)} %collective-permute-done.1.refs_11_), channel_id=1, source_target_pairs={{0,32},{1,33},{2,34},{3,35},{4,36},{5,37},{6,38},{7,39},{8,40},{9,... | collective-permute-start | bytes 1179656 | tf_op jit(solution)/shard_map/ppermute | solution.py:329
  43.4 14.8 %collective-permute-start.6 = (bf16[512,384]{1,0:T(8,128)(2,1)S(1)}, bf16[512,384]{1,0:T(8,128)(2,1)S(1)}, u32[]{:S(2)}, u32[]{:S(2)}) collective-permute-start(bf16[512,384]{1,0:T(8,128)(2,1)S(1)} %collective-permute-done.5.refs_12_), channel_id=1, source_target_pairs={{0,224},{1,225},{2,226},{3,227},{4,228},{5,229},{6,230},{7,231},{8... | collective-permute-start | bytes 1179656 | tf_op jit(solution)/shard_map/ppermute | solution.py:330
  52.5 14.2 %collective-permute-start.3 = (bf16[512,384]{1,0:T(8,128)(2,1)S(1)}, bf16[512,384]{1,0:T(8,128)(2,1)S(1)}, u32[]{:S(2)}, u32[]{:S(2)}) collective-permute-start(bf16[512,384]{1,0:T(8,128)(2,1)S(1)} %collective-permute-done.2.refs_13_), channel_id=1, source_target_pairs={{0,32},{1,33},{2,34},{3,35},{4,36},{5,37},{6,38},{7,39},{8,40},{9,... | collective-permute-start | bytes 1179656 | tf_op jit(solution)/shard_map/ppermute | solution.py:329
  58.2 21.8 %collective-permute-start.7 = (bf16[512,384]{1,0:T(8,128)(2,1)S(1)}, bf16[512,384]{1,0:T(8,128)(2,1)S(1)}, u32[]{:S(2)}, u32[]{:S(2)}) collective-permute-start(bf16[512,384]{1,0:T(8,128)(2,1)S(1)} %collective-permute-done.6.refs_14_), channel_id=1, source_target_pairs={{0,224},{1,225},{2,226},{3,227},{4,228},{5,229},{6,230},{7,231},{8... | collective-permute-start | bytes 1179656 | tf_op jit(solution)/shard_map/ppermute | solution.py:330
  66.8 16.5 %collective-permute-start.4 = (bf16[512,384]{1,0:T(8,128)(2,1)S(1)}, bf16[512,384]{1,0:T(8,128)(2,1)S(1)}, u32[]{:S(2)}, u32[]{:S(2)}) collective-permute-start(bf16[512,384]{1,0:T(8,128)(2,1)S(1)} %collective-permute-done.3.refs_4_), channel_id=1, source_target_pairs={{0,32},{1,33},{2,34},{3,35},{4,36},{5,37},{6,38},{7,39},{8,40},{9,... | collective-permute-start | bytes 1179656 | tf_op jit(solution)/shard_map/ppermute | solution.py:331
  85.5 3.2 %collective-permute-start.9 = (bf16[512,128]{1,0:T(8,128)(2,1)S(1)}, bf16[512,128]{1,0:T(8,128)(2,1)S(1)}, u32[]{:S(2)}, u32[]{:S(2)}) collective-permute-start(bf16[512,128]{1,0:T(8,128)(2,1)S(1)} %get-tuple-element.31), channel_id=1, source_target_pairs={{0,256},{256,0},{1,257},{257,1},{2,258},{258,2},{3,259},{259,3},{4... | collective-permute-start | bytes 393224 | tf_op jit(solution)/shard_map/ppermute | solution.py:38
  88.8 14.6 %collective-permute-start.10 = (bf16[512,256]{1,0:T(8,128)(2,1)S(1)}, bf16[512,256]{1,0:T(8,128)(2,1)S(1)}, u32[]{:S(2)}, u32[]{:S(2)}) collective-permute-start(bf16[512,256]{1,0:T(8,128)(2,1)S(1)} %pad_maximum_fusion.2.own), channel_id=1, source_target_pairs={{0,8},{1,9},{2,10},{3,11},{4,12},{5,13},{6,14},{7,15},{8,16},{9,17... | collective-permute-start | bytes 786440 | tf_op jit(solution)/shard_map/ppermute | solution.py:348
  96.3 9.2 %collective-permute-start.8 = (bf16[512,256]{1,0:T(8,128)(2,1)}, bf16[512,256]{1,0:T(8,128)(2,1)S(1)}, u32[]{:S(2)}, u32[]{:S(2)}) collective-permute-start(bf16[512,256]{1,0:T(8,128)(2,1)} %get-tuple-element.29), channel_id=1, source_target_pairs={{0,256},{256,0},{1,257},{257,1},{2,258},{258,2},{3,259},{259,3},{4... | collective-permute-start | bytes 786440 | tf_op jit(solution)/shard_map/ppermute | solution.py:38
  98.2 19.1 %collective-permute-start.12 = (bf16[512,256]{1,0:T(8,128)(2,1)S(1)}, bf16[512,256]{1,0:T(8,128)(2,1)S(1)}, u32[]{:S(2)}, u32[]{:S(2)}) collective-permute-start(bf16[512,256]{1,0:T(8,128)(2,1)S(1)} %pad_maximum_fusion.2.own), channel_id=1, source_target_pairs={{0,24},{1,25},{2,26},{3,27},{4,28},{5,29},{6,30},{7,31},{8,32},{9,... | collective-permute-start | bytes 786440 | tf_op jit(solution)/shard_map/ppermute | solution.py:349
  103.5 18.7 %collective-permute-start.11 = (bf16[512,256]{1,0:T(8,128)(2,1)S(1)}, bf16[512,256]{1,0:T(8,128)(2,1)S(1)}, u32[]{:S(2)}, u32[]{:S(2)}) collective-permute-start(bf16[512,256]{1,0:T(8,128)(2,1)S(1)} %collective-permute-done.10.one_three), channel_id=1, source_target_pairs={{0,8},{1,9},{2,10},{3,11},{4,12},{5,13},{6,14},{7,15},{8,16},{9,17... | collective-permute-start | bytes 786440 | tf_op jit(solution)/shard_map/ppermute | solution.py:350

commit v2 on v1

--- a/solution.py
+++ b/solution.py
@@ -48,91 +48,86 @@
     return values * cosine + pltpu.roll(values, values.shape[-1] // 2, 1) * sine
 
 
-def part_kernel(order, *refs, alone, both, carried):
+def part_kernel(order, *refs, plan):
     refs = list(refs)
     take = lambda count: [refs.pop(0) for _ in range(count)]
-    mine, other = take(alone + both), take(both)
-    weights = take(alone + both)
-    totals = take(2) if carried else None
-    out_mine, out_other = refs
-    sums = [totals[0][...], totals[1][...]] if carried else [0.0, 0.0]
-    for i, weight in enumerate(weights):
-        sums[0] = sums[0] + jnp.dot(
-            mine[i][...], weight[...], preferred_element_type=jnp.float32
-        )
-        if i >= alone:
-            sums[1] = sums[1] + jnp.dot(
-                other[i - alone][...], weight[...], preferred_element_type=jnp.float32
-            )
-    out_mine[...] = sums[0]
-    out_other[...] = sums[1]
-
-
-def project_part(order, mine, other, alone, both, totals, name):
-    rows = mine.shape[0]
+    weights = take(1 + max(max(use) for use, _ in plan))
+    inputs = [(take(len(use)), use, take(int(carried))) for use, carried in plan]
+    for (tokens, use, carried), out in zip(inputs, refs):
+        total = carried[0][...] if carried else 0.0
+        for part, i in zip(tokens, use):
+            total = total + jnp.dot(part[...], weights[i][...], preferred_element_type=jnp.float32)
+        out[...] = total
+
+
+def project_part(order, blocks, results, name):
+    rows = results[0][0].shape[0]
     steps = 2
     part = rows // steps
-    weights = alone + both
-    depth, columns = weights[0].shape
+    depth, columns = blocks[0].shape
     tokens = lambda place: pl.BlockSpec((part, depth), lambda i, order: (i, order[place]))
     out = pl.BlockSpec((part, columns), lambda i, order: (i, 0))
-    places = list(range(len(weights)))
-    work = 2 * rows * depth * columns * (len(alone) + 2 * len(both))
+    specs = [pl.BlockSpec((depth, columns), lambda i, order: (0, 0))] * len(blocks)
+    args = list(blocks)
+    for source, use, carried in results:
+        specs += [tokens(place) for place in use] + [out] * (carried is not None)
+        args += [source] * len(use) + [carried] * (carried is not None)
+    work = 2 * rows * depth * columns * sum(len(use) for _, use, _ in results)
     return pl.pallas_call(
         functools.partial(
-            part_kernel, alone=len(alone), both=len(both), carried=bool(totals)
+            part_kernel, plan=[(use, carried is not None) for _, use, carried in results]
         ),
         grid_spec=pltpu.PrefetchScalarGridSpec(
             num_scalar_prefetch=1,
             grid=(steps,),
-            in_specs=[tokens(place) for place in places + places[len(alone) :]]
-            + [pl.BlockSpec((depth, columns), lambda i, order: (0, 0))] * len(weights)
-            + [out] * len(totals),
-            out_specs=[out, out],
-        ),
-        out_shape=[jax.ShapeDtypeStruct((rows, columns), jnp.float32)] * 2,
+            in_specs=specs,
+            out_specs=[out] * len(results),
+        ),
+        out_shape=[jax.ShapeDtypeStruct((rows, columns), jnp.float32)] * len(results),
         compiler_params=pltpu.CompilerParams(vmem_limit_bytes=vmem_bytes),
         cost_estimate=pl.CostEstimate(
             flops=work, bytes_accessed=work // 256, transcendentals=0
         ),
         name=name,
-    )(order, *[mine] * len(weights), *[other] * len(both), *weights, *totals)
+    )(order, *args)
 
 
 def finish_kernel(
-    scalars, mine, other, weight, total_mine, total_other, cosine, sine, out_mine, out_other, *, part
+    scalars, mine, other, weight, total_mine, total_other, cosine, sine, out_mine, out_other
 ):
     head_dim = cosine.shape[1]
+    heads = weight.shape[1] // head_dim
     for source, total, out in ((mine, total_mine, out_mine), (other, total_other, out_other)):
         value = total[...] + jnp.dot(
             source[...], weight[...], preferred_element_type=jnp.float32
         )
-        for head in range(out.shape[1] // head_dim):
+        for head in range(heads):
             columns = slice(head * head_dim, (head + 1) * head_dim)
             turned = rotated(value[:, columns], cosine[...], sine[...])
-            if part == "kv":
+            if head == heads - 1:
                 turned = jnp.where(scalars[1] == 0, turned, value[:, columns])
             out[:, columns] = turned.astype(out.dtype)
 
 
-def finish(scalars, mine, other, weight, totals, cosine, sine, columns, place, part):
-    rows, depth = mine.shape[0], weight.shape[0]
+def finish(scalars, mine, other, weight, totals, cosine, sine):
+    rows, (depth, columns) = mine.shape[0], weight.shape
+    steps = 2
+    part = rows // steps
     head_dim = cosine.shape[1]
-    tokens = pl.BlockSpec((rows, depth), lambda i, scalars: (0, scalars[0]))
-    total = pl.BlockSpec((rows, columns), lambda i, scalars: (0, place))
-    table = pl.BlockSpec((rows, head_dim), lambda i, scalars: (0, 0))
-    out = pl.BlockSpec((rows, columns), lambda i, scalars: (0, 0))
+    tokens = pl.BlockSpec((part, depth), lambda i, scalars: (i, scalars[0]))
+    table = pl.BlockSpec((part, head_dim), lambda i, scalars: (i, 0))
+    out = pl.BlockSpec((part, columns), lambda i, scalars: (i, 0))
     return pl.pallas_call(
-        functools.partial(finish_kernel, part=part),
+        finish_kernel,
         grid_spec=pltpu.PrefetchScalarGridSpec(
             num_scalar_prefetch=1,
-            grid=(1,),
+            grid=(steps,),
             in_specs=[
                 tokens,
                 tokens,
-                pl.BlockSpec((depth, columns), lambda i, scalars: (0, place)),
-                total,
-                total,
+                pl.BlockSpec((depth, columns), lambda i, scalars: (0, 0)),
+                out,
+                out,
                 table,
                 table,
             ],
@@ -145,7 +140,7 @@
             bytes_accessed=4 * rows * depth + 8 * rows * columns,
             transcendentals=0,
         ),
-        name=part + "_finish",
+        name="finish",
     )(scalars, mine, other, weight, *totals, cosine, sine)
 
 
@@ -245,11 +240,12 @@
             ]
 
 
-def attend(core, q_mine, q_other, one_three, three_one, two, own, starts):
-    rows, columns = q_mine.shape
+def attend(core, q_mine, q_other, columns, one_three, three_one, two, own, starts):
+    rows = own.shape[0]
     head_dim = own.shape[1] // 2
     height = rows * columns // head_dim
     whole = lambda array: pl.BlockSpec(array.shape, lambda i, core: (0, 0))
+    half = pl.BlockSpec((rows, columns), lambda i, core: (0, 0))
     args = (q_mine, q_other, one_three, three_one, own, starts)
     kept = pl.BlockSpec((height, head_dim), lambda i, core: (i, 0))
     partial, stats = pl.pallas_call(
@@ -257,7 +253,7 @@
         grid_spec=pltpu.PrefetchScalarGridSpec(
             num_scalar_prefetch=1,
             grid=(2,),
-            in_specs=[whole(array) for array in args],
+            in_specs=[half, half] + [whole(array) for array in args[2:]],
             out_specs=[kept, kept],
             scratch_shapes=[pltpu.VMEM(own.shape, own.dtype)] * 2,
         ),
@@ -276,7 +272,7 @@
         grid_spec=pltpu.PrefetchScalarGridSpec(
             num_scalar_prefetch=1,
             grid=(2,),
-            in_specs=[whole(array) for array in args] + [kept, kept],
+            in_specs=[half, half] + [whole(array) for array in args[2:]] + [kept, kept],
             out_specs=pl.BlockSpec((rows, columns), lambda i, core: (0, (i + core[0]) % 2)),
         ),
         out_shape=jax.ShapeDtypeStruct((rows, 2 * columns), jnp.bfloat16),
@@ -324,24 +320,33 @@
     )
     tokens_other = swap_cores(tokens)
     ahead, back = ring_pairs(lambda dp: 1 - 2 * dp), ring_pairs(lambda dp: 2 * dp - 1)
-    aheads, backs = [block], [block]
-    for _ in range(z_size // 2 - 1):
-        aheads.append(lax.ppermute(aheads[-1], axes, ahead))
-        backs.append(lax.ppermute(backs[-1], axes, back))
-    far = lax.ppermute(aheads[-1], axes, ahead)
-    blocks = [block] + [part for pair in zip(aheads[1:], backs[1:]) for part in pair]
+    send_ahead = lambda value: lax.ppermute(value, axes, ahead)
+    send_back = lambda value: lax.ppermute(value, axes, back)
     steps = jnp.array([0, -1, 1, -2, 2, -3, 3, 4], jnp.int32)
     order = (plane + steps * (1 - 2 * core)) % z_size
-    totals = project_part(order[:5], tokens, tokens_other, [], blocks[:5], [], "near")
+    ahead1, back1 = send_ahead(block), send_back(block)
+    ahead2, back2 = send_ahead(ahead1), send_back(back1)
+    blocks = [block, ahead1, back1]
+    (total,) = project_part(order, blocks, [(tokens, [0, 1, 2], None)], "first")
+    ahead2, total = lax.optimization_barrier((ahead2, total))
+    ahead3, back3 = send_ahead(ahead2), send_back(back2)
+    blocks += [ahead2, back2]
     totals = project_part(
-        order[5:7], tokens, tokens_other, [], blocks[5:], list(totals), "farther"
-    )
-
-    scalars = jnp.stack([order[-1], core])
-    last = (scalars, tokens, tokens_other, far, totals, cosine, sine)
-    kv_mine, kv_theirs = finish(*last, head_dim, half_cols // head_dim, "kv")
-    kv_other = swap_cores(kv_theirs)
+        order, blocks, [(tokens, [3, 4], total), (tokens_other, [0, 1, 2, 3, 4], None)], "second"
+    )
+    ahead3, *totals = lax.optimization_barrier((ahead3, *totals))
+    far = send_ahead(ahead3)
+    totals = project_part(
+        order[5:7],
+        [ahead3, back3],
+        [(tokens, [0, 1], totals[0]), (tokens_other, [0, 1], totals[1])],
+        "third",
+    )
+    scalars = jnp.stack([order[7], core])
+    mine, theirs = finish(scalars, tokens, tokens_other, far, totals, cosine, sine)
+    other = swap_cores(theirs)
     first = core == 0
+    kv_mine, kv_other = mine[:, half_cols:], other[:, half_cols:]
     own = jnp.concatenate(
         [lax.select(first, kv_mine, kv_other), lax.select(first, kv_other, kv_mine)], axis=1
     )
@@ -349,9 +354,7 @@
     three_one = lax.ppermute(own, axes, shift_pairs(lambda dp: 3 - 2 * dp))
     two = lax.ppermute(one_three, axes, shift_pairs(lambda dp: 1 - 2 * dp))
     core_index = core.reshape(1).astype(jnp.int32)
-    q_mine, q_theirs = finish(*last, half_cols, 0, "q")
-    q_other = swap_cores(q_theirs)
-    out = attend(core_index, q_mine, q_other, one_three, three_one, two, own, starts)
+    out = attend(core_index, mine, other, half_cols, one_three, three_one, two, own, starts)
     return out[:, None]
 
 

time: 127 us -> 124 us (0.976)
  the two profiles are of different devices: /device:TPU:196 before, /device:TPU:260 now
where the time goes in v2:
time: 124 us
  waiting for transfers between devices  50.7 us (41%)
  starting transfers between devices  42.2 us (34%)
  Pallas kernels  21.5 us (17%)
  local copies, waits for them, and re-layouts  5.44 us (4%)
  other arithmetic  3.6 us (3%)
    ppermute x4, waiting for transfers between devices, per_device(): send_ahead = lambda value: lax.ppermute(value, axes, ahead)  16.5 us
    ppermute x1, waiting for transfers between devices, per_device(): one_three = lax.ppermute(own, axes, shift_pairs(lambda dp: 1 + 2 * dp))  16.4 us
    ppermute x3, starting transfers between devices, per_device(): send_back = lambda value: lax.ppermute(value, axes, back)  13.9 us
    all_to_all x1, waiting for transfers between devices, spread(): parts = lax.all_to_all(copies, axis, 0, 0)  10.6 us
    pallas_call x3, Pallas kernels, project_part(): pl.pallas_call(functools.partial(part_kernel, plan=[(use, carried is not...  9.56 us
    ppermute x4, starting transfers between devices, per_device(): send_ahead = lambda value: lax.ppermute(value, axes, ahead)  9.11 us
    all_to_all x1, starting transfers between devices, spread(): parts = lax.all_to_all(copies, axis, 0, 0)  7.09 us
    ppermute x1, waiting for transfers between devices, per_device(): two = lax.ppermute(one_three, axes, shift_pairs(lambda dp: 1 - 2 * dp))  5.56 us
  transfers between devices with their start and end apart: 13, of which 8 were waited for; matrix products, arithmetic and copies ran while one was open for 4% of the time, Pallas kernels for 12%

profile of v2, /device:TPU:260, one launch (start us, length us, event | category | flops | bytes accessed | tf_op | source)
XLA Modules:
  0.0 123.7 jit_solution(9522817443511194603)
XLA Ops:
  0.0 0.0 copy-start
  0.0 0.9 copy-done
  0.9 0.8 dynamic-slice_bitcast_fusion.1
  1.7 0.8 broadcast_in_dim.22
  2.5 7.1 %all-to-all-start = ((bf16[4,128,384]{2,1,0:T(8,128)(2,1)}), bf16[4,128,384]{2,1,0:T(8,128)(2,1)S(1)}, u32[]{:S(2)}, u32[]{:S(2)}) async-start(bf16[4,128,384]{2,1,0:T(8,128)(2,1)} %broadcast_in_dim.22), calls=%async_computation | async-start | bytes 786432 | tf_op jit(solution)/shard_map/all_to_all | solution.py:43
  9.6 1.0 fusion
  10.6 0.8 select_reduce_fusion.1
  11.4 0.1 select_reduce_fusion
  11.5 0.1 pad_maximum_fusion.cosine
  11.6 0.1 pad_maximum_fusion.1.sine
  11.8 10.6 %all-to-all-done = bf16[4,128,384]{2,1,0:T(8,128)(2,1)S(1)} async-done(((bf16[4,128,384]{2,1,0:T(8,128)(2,1)}), bf16[4,128,384]{2,1,0:T(8,128)(2,1)S(1)}, u32[]{:S(2)}, u32[]{:S(2)}) %all-to-all-start) | async-done | bytes 393248 | tf_op jit(solution)/shard_map/all_to_all | solution.py:43
  22.4 1.9 %collective-permute-start = (bf16[512,4096]{1,0:T(8,128)(2,1)}, bf16[512,4096]{1,0:T(8,128)(2,1)}, u32[]{:S(2)}, u32[]{:S(2)}) collective-permute-start(bf16[512,4096]{1,0:T(8,128)(2,1)} %mine), channel_id=1, source_target_pairs={{0,256},{256,0},{1,257},{257,1},{2,258},{258,2},{3,259},{259,3},{4... | collective-permute-start | bytes 12582920 | tf_op jit(solution)/shard_map/ppermute | solution.py:38
  24.3 3.4 %collective-permute-start.1 = (bf16[512,384]{1,0:T(8,128)(2,1)S(1)}, bf16[512,384]{1,0:T(8,128)(2,1)S(1)}, u32[]{:S(2)}, u32[]{:S(2)}) collective-permute-start(bf16[512,384]{1,0:T(8,128)(2,1)S(1)} %bitcast.8), channel_id=1, source_target_pairs={{0,32},{1,33},{2,34},{3,35},{4,36},{5,37},{6,38},{7,39},{8,40},{9,... | collective-permute-start | bytes 1179656 | tf_op jit(solution)/shard_map/ppermute | solution.py:323
  27.7 3.7 %collective-permute-start.3 = (bf16[512,384]{1,0:T(8,128)(2,1)S(1)}, bf16[512,384]{1,0:T(8,128)(2,1)S(1)}, u32[]{:S(2)}, u32[]{:S(2)}) collective-permute-start(bf16[512,384]{1,0:T(8,128)(2,1)S(1)} %bitcast.9), channel_id=1, source_target_pairs={{0,224},{1,225},{2,226},{3,227},{4,228},{5,229},{6,230},{7,231},{8... | collective-permute-start | bytes 1179656 | tf_op jit(solution)/shard_map/ppermute | solution.py:324
  31.3 6.5 %collective-permute-done.1.refs_1_ = bf16[512,384]{1,0:T(8,128)(2,1)S(1)} collective-permute-done((bf16[512,384]{1,0:T(8,128)(2,1)S(1)}, bf16[512,384]{1,0:T(8,128)(2,1)S(1)}, u32[]{:S(2)}, u32[]{:S(2)}) %collective-permute-start.1) | collective-permute-done | bytes 393248 | tf_op jit(solution)/shard_map/ppermute | solution.py:323
  37.9 1.9 %collective-permute-start.2 = (bf16[512,384]{1,0:T(8,128)(2,1)S(1)}, bf16[512,384]{1,0:T(8,128)(2,1)S(1)}, u32[]{:S(2)}, u32[]{:S(2)}) collective-permute-start(bf16[512,384]{1,0:T(8,128)(2,1)S(1)} %collective-permute-done.1.refs_1_), channel_id=1, source_target_pairs={{0,32},{1,33},{2,34},{3,35},{4,36},{5,37},{6,38},{7,39},{8,40},{9,... | collective-permute-start | bytes 1179656 | tf_op jit(solution)/shard_map/ppermute | solution.py:323
  39.8 0.0 collective-permute-done.3.refs_2_
  39.8 5.1 %collective-permute-start.5 = (bf16[512,384]{1,0:T(8,128)(2,1)S(1)}, bf16[512,384]{1,0:T(8,128)(2,1)S(1)}, u32[]{:S(2)}, u32[]{:S(2)}) collective-permute-start(bf16[512,384]{1,0:T(8,128)(2,1)S(1)} %collective-permute-done.3.refs_2_), channel_id=1, source_target_pairs={{0,224},{1,225},{2,226},{3,227},{4,228},{5,229},{6,230},{7,231},{8... | collective-permute-start | bytes 1179656 | tf_op jit(solution)/shard_map/ppermute | solution.py:324
  44.9 0.7 and_select_fusion.order
  45.6 0.0 copy-start.1
  45.6 2.2 %copy-done.1 = bf16[512,4096]{1,0:T(8,128)(2,1)S(1)} copy-done((bf16[512,4096]{1,0:T(8,128)(2,1)S(1)}, bf16[512,4096]{1,0:T(8,128)(2,1)}, u32[]{:S(2)}) %copy-start.1) | copy-done | bytes 4194328
  47.8 1.9 %first.1.refs_7_ = f32[512,384]{1,0:T(8,128)S(1)} custom-call(s32[8]{0:T(128)S(1)} %and_select_fusion.order, bf16[512,384]{1,0:T(8,128)(2,1)S(1)} %bitcast.10, bf16[512,384]{1,0:T(8,128)(2,1)S(1)} %collective-permute-done.1.refs_1_, bf16[512,384]{1,0:T(8,128)(2,1)S(1)} %collective-permute-done.3.refs_2_, bf16[512,4096]{1,0:T(8,128)(2,1)S(1)} %copy-done.1, ...), custom_call_target="tpu_custom_call" | custom-call | flops 603979776 | bytes 2359296 | tf_op jit(solution)/shard_map/first/pallas_call | solution.py:76
  49.7 3.0 %collective-permute-done.2.refs_3_ = bf16[512,384]{1,0:T(8,128)(2,1)S(1)} collective-permute-done((bf16[512,384]{1,0:T(8,128)(2,1)S(1)}, bf16[512,384]{1,0:T(8,128)(2,1)S(1)}, u32[]{:S(2)}, u32[]{:S(2)}) %collective-permute-start.2) | collective-permute-done | bytes 393248 | tf_op jit(solution)/shard_map/ppermute | solution.py:323
  52.7 1.9 %collective-permute-start.4 = (bf16[512,384]{1,0:T(8,128)(2,1)S(1)}, bf16[512,384]{1,0:T(8,128)(2,1)S(1)}, u32[]{:S(2)}, u32[]{:S(2)}) collective-permute-start(bf16[512,384]{1,0:T(8,128)(2,1)S(1)} %collective-permute-done.2.refs_3_), channel_id=1, source_target_pairs={{0,32},{1,33},{2,34},{3,35},{4,36},{5,37},{6,38},{7,39},{8,40},{9,... | collective-permute-start | bytes 1179656 | tf_op jit(solution)/shard_map/ppermute | solution.py:323
  54.6 0.0 collective-permute-done.5.refs_4_
  54.6 5.1 %collective-permute-start.7 = (bf16[512,384]{1,0:T(8,128)(2,1)S(1)}, bf16[512,384]{1,0:T(8,128)(2,1)S(1)}, u32[]{:S(2)}, u32[]{:S(2)}) collective-permute-start(bf16[512,384]{1,0:T(8,128)(2,1)S(1)} %collective-permute-done.5.refs_4_), channel_id=1, source_target_pairs={{0,224},{1,225},{2,226},{3,227},{4,228},{5,229},{6,230},{7,231},{8... | collective-permute-start | bytes 1179656 | tf_op jit(solution)/shard_map/ppermute | solution.py:324
  59.7 0.0 collective-permute-done.refs_8_.refs_9_.refs_10_.refs_11_.refs_12_.refs_5_.refs_6_.other
  59.7 4.5 %second.1 = (f32[512,384]{1,0:T(8,128)S(1)}, f32[512,384]{1,0:T(8,128)S(1)}) custom-call(s32[8]{0:T(128)S(1)} %and_select_fusion.order, bf16[512,384]{1,0:T(8,128)(2,1)S(1)} %bitcast.11, bf16[512,384]{1,0:T(8,128)(2,1)S(1)} %collective-permute-done.1.refs_1_, bf16[512,384]{1,0:T(8,128)(2,1)S(1)} %collective-permute-done.3.refs_2_, ...), custom_call_target="tpu_custom_call" | custom-call | flops 1409286144 | bytes 5505024 | tf_op jit(solution)/shard_map/second/pallas_call | solution.py:76
  64.2 2.7 %collective-permute-done.4.refs_0_ = bf16[512,384]{1,0:T(8,128)(2,1)S(1)} collective-permute-done((bf16[512,384]{1,0:T(8,128)(2,1)S(1)}, bf16[512,384]{1,0:T(8,128)(2,1)S(1)}, u32[]{:S(2)}, u32[]{:S(2)}) %collective-permute-start.4) | collective-permute-done | bytes 393248 | tf_op jit(solution)/shard_map/ppermute | solution.py:323
  66.9 1.9 %collective-permute-start.6 = (bf16[512,384]{1,0:T(8,128)(2,1)S(1)}, bf16[512,384]{1,0:T(8,128)(2,1)S(1)}, u32[]{:S(2)}, u32[]{:S(2)}) collective-permute-start(bf16[512,384]{1,0:T(8,128)(2,1)S(1)} %collective-permute-done.4.refs_0_), channel_id=1, source_target_pairs={{0,32},{1,33},{2,34},{3,35},{4,36},{5,37},{6,38},{7,39},{8,40},{9,... | collective-permute-start | bytes 1179656 | tf_op jit(solution)/shard_map/ppermute | solution.py:323
  68.8 0.1 slice.13.order
  68.9 0.6 slice.12
  69.5 0.7 pad_add_fusion.scalars
  70.2 0.0 collective-permute-done.7.refs_1_
  70.2 3.2 %third.1 = (f32[512,384]{1,0:T(8,128)S(1)}, f32[512,384]{1,0:T(8,128)S(1)}) custom-call(s32[2]{0:T(128)S(1)} %slice.13.order, bf16[512,384]{1,0:T(8,128)(2,1)S(1)} %collective-permute-done.4.refs_0_, bf16[512,384]{1,0:T(8,128)(2,1)S(1)} %collective-permute-done.7.refs_1_, bf16[512,4096]{1,0:T(8,128)(2,1)} %mine, bf16[512,4096]{1,0:T(8,128)(2,1)} %mine, ...), custom_call_target="tpu_custom_call" | custom-call | flops 805306368 | bytes 3145728 | tf_op jit(solution)/shard_map/third/pallas_call | solution.py:76
  73.4 4.3 %collective-permute-done.6.weight = bf16[512,384]{1,0:T(8,128)(2,1)S(1)} collective-permute-done((bf16[512,384]{1,0:T(8,128)(2,1)S(1)}, bf16[512,384]{1,0:T(8,128)(2,1)S(1)}, u32[]{:S(2)}, u32[]{:S(2)}) %collective-permute-start.6) | collective-permute-done | bytes 393248 | tf_op jit(solution)/shard_map/ppermute | solution.py:323
  77.8 2.7 %finish.1 = (bf16[512,384]{1,0:T(8,128)(2,1)S(1)}, bf16[512,384]{1,0:T(8,128)(2,1)S(1)}) custom-call(s32[2]{0:T(128)S(1)} %pad_add_fusion.scalars, bf16[512,4096]{1,0:T(8,128)(2,1)} %mine, bf16[512,4096]{1,0:T(8,128)(2,1)} %collective-permute-done.refs_8_.refs_9_.refs_10_.refs_11_.refs_12_.refs_5_.refs_6_.other, ...), custom_call_target="tpu_custom_call" | custom-call | flops 402653184 | bytes 2621440 | tf_op jit(solution)/shard_map/finish/pallas_call | solution.py:120
  80.5 1.9 %collective-permute-start.8 = (bf16[512,384]{1,0:T(8,128)(2,1)S(1)}, bf16[512,384]{1,0:T(8,128)(2,1)S(1)}, u32[]{:S(2)}, u32[]{:S(2)}) collective-permute-start(bf16[512,384]{1,0:T(8,128)(2,1)S(1)} %get-tuple-element.37), channel_id=1, source_target_pairs={{0,256},{256,0},{1,257},{257,1},{2,258},{258,2},{3,259},{259,3},{4... | collective-permute-start | bytes 1179656 | tf_op jit(solution)/shard_map/ppermute | solution.py:38
  82.4 1.7 %collective-permute-done.8.q_other = bf16[512,384]{1,0:T(8,128)(2,1)S(1)} collective-permute-done((bf16[512,384]{1,0:T(8,128)(2,1)S(1)}, bf16[512,384]{1,0:T(8,128)(2,1)S(1)}, u32[]{:S(2)}, u32[]{:S(2)}) %collective-permute-start.8) | collective-permute-done | bytes 393248 | tf_op jit(solution)/shard_map/ppermute | solution.py:38
  84.2 4.4 %collective-permute-start.9 = (bf16[512,256]{1,0:T(8,128)(2,1)S(1)}, bf16[512,256]{1,0:T(8,128)(2,1)S(1)}, u32[]{:S(2)}, u32[]{:S(2)}) collective-permute-start(bf16[512,256]{1,0:T(8,128)(2,1)S(1)} %pad_maximum_fusion.2.own), channel_id=1, source_target_pairs={{0,8},{1,9},{2,10},{3,11},{4,12},{5,13},{6,14},{7,15},{8,16},{9,17... | collective-permute-start | bytes 786440 | tf_op jit(solution)/shard_map/ppermute | solution.py:353
  88.5 1.9 %collective-permute-start.11 = (bf16[512,256]{1,0:T(8,128)(2,1)S(1)}, bf16[512,256]{1,0:T(8,128)(2,1)S(1)}, u32[]{:S(2)}, u32[]{:S(2)}) collective-permute-start(bf16[512,256]{1,0:T(8,128)(2,1)S(1)} %pad_maximum_fusion.2.own), channel_id=1, source_target_pairs={{0,24},{1,25},{2,26},{3,27},{4,28},{5,29},{6,30},{7,31},{8,32},{9,... | collective-permute-start | bytes 786440 | tf_op jit(solution)/shard_map/ppermute | solution.py:354
  90.5 16.4 %collective-permute-done.9.one_three = bf16[512,256]{1,0:T(8,128)(2,1)S(1)} collective-permute-done((bf16[512,256]{1,0:T(8,128)(2,1)S(1)}, bf16[512,256]{1,0:T(8,128)(2,1)S(1)}, u32[]{:S(2)}, u32[]{:S(2)}) %collective-permute-start.9) | collective-permute-done | bytes 262176 | tf_op jit(solution)/shard_map/ppermute | solution.py:353
  106.8 1.9 %collective-permute-start.10 = (bf16[512,256]{1,0:T(8,128)(2,1)S(1)}, bf16[512,256]{1,0:T(8,128)(2,1)S(1)}, u32[]{:S(2)}, u32[]{:S(2)}) collective-permute-start(bf16[512,256]{1,0:T(8,128)(2,1)S(1)} %collective-permute-done.9.one_three), channel_id=1, source_target_pairs={{0,8},{1,9},{2,10},{3,11},{4,12},{5,13},{6,14},{7,15},{8,16},{9,17... | collective-permute-start | bytes 786440 | tf_op jit(solution)/shard_map/ppermute | solution.py:355
  108.7 0.1 copy.9.starts
  108.9 0.0 collective-permute-done.11.three_one
  108.9 4.8 %attend_near.1 = (f32[2048,128]{1,0:T(8,128)S(1)}, f32[2048,128]{1,0:T(8,128)S(1)}) custom-call(s32[1]{0:T(128)} %bitcast.core, bf16[512,384]{1,0:T(8,128)(2,1)S(1)} %get-tuple-element.36.q_mine, bf16[512,384]{1,0:T(8,128)(2,1)S(1)} %collective-permute-done.8.q_other, bf16[512,256]{1,0:T(8,128)(2,1)S(1)} %collective-permute-done.9.one_three, ...), custom_call_target="tpu_custom_call" | custom-call | flops 1207959552 | bytes 2097152 | tf_op jit(solution)/shard_map/attend_near/pallas_call | solution.py:251
  113.7 5.6 %collective-permute-done.10.two = bf16[512,256]{1,0:T(8,128)(2,1)S(1)} collective-permute-done((bf16[512,256]{1,0:T(8,128)(2,1)S(1)}, bf16[512,256]{1,0:T(8,128)(2,1)S(1)}, u32[]{:S(2)}, u32[]{:S(2)}) %collective-permute-start.10) | collective-permute-done | bytes 262176 | tf_op jit(solution)/shard_map/ppermute | solution.py:355
  119.3 4.4 %attend_last.1 = bf16[512,512]{1,0:T(8,128)(2,1)} custom-call(s32[1]{0:T(128)} %bitcast.core, bf16[512,384]{1,0:T(8,128)(2,1)S(1)} %get-tuple-element.36.q_mine, bf16[512,384]{1,0:T(8,128)(2,1)S(1)} %collective-permute-done.8.q_other, bf16[512,256]{1,0:T(8,128)(2,1)S(1)} %collective-permute-done.10.two, s32[512,1]{1,0:T(8,128)S(1)} %copy.9.starts, ...), custom_call_target="tpu_custom_call" | custom-call | flops 536870912 | bytes 2097152 | tf_op jit(solution)/shard_map/attend_last/pallas_call | solution.py:270
  (7 shorter events, 0.1 us)
Async XLA Ops:
  0.0 0.9 copy-start
  2.5 19.9 %all-to-all-start = ((bf16[4,128,384]{2,1,0:T(8,128)(2,1)}), bf16[4,128,384]{2,1,0:T(8,128)(2,1)S(1)}, u32[]{:S(2)}, u32[]{:S(2)}) async-start(bf16[4,128,384]{2,1,0:T(8,128)(2,1)} %broadcast_in_dim.22), calls=%async_computation | async-start | bytes 786432 | tf_op jit(solution)/shard_map/all_to_all | solution.py:43
  22.4 37.4 %collective-permute-start = (bf16[512,4096]{1,0:T(8,128)(2,1)}, bf16[512,4096]{1,0:T(8,128)(2,1)}, u32[]{:S(2)}, u32[]{:S(2)}) collective-permute-start(bf16[512,4096]{1,0:T(8,128)(2,1)} %mine), channel_id=1, source_target_pairs={{0,256},{256,0},{1,257},{257,1},{2,258},{258,2},{3,259},{259,3},{4... | collective-permute-start | bytes 12582920 | tf_op jit(solution)/shard_map/ppermute | solution.py:38
  24.3 13.6 %collective-permute-start.1 = (bf16[512,384]{1,0:T(8,128)(2,1)S(1)}, bf16[512,384]{1,0:T(8,128)(2,1)S(1)}, u32[]{:S(2)}, u32[]{:S(2)}) collective-permute-start(bf16[512,384]{1,0:T(8,128)(2,1)S(1)} %bitcast.8), channel_id=1, source_target_pairs={{0,32},{1,33},{2,34},{3,35},{4,36},{5,37},{6,38},{7,39},{8,40},{9,... | collective-permute-start | bytes 1179656 | tf_op jit(solution)/shard_map/ppermute | solution.py:323
  27.7 12.1 %collective-permute-start.3 = (bf16[512,384]{1,0:T(8,128)(2,1)S(1)}, bf16[512,384]{1,0:T(8,128)(2,1)S(1)}, u32[]{:S(2)}, u32[]{:S(2)}) collective-permute-start(bf16[512,384]{1,0:T(8,128)(2,1)S(1)} %bitcast.9), channel_id=1, source_target_pairs={{0,224},{1,225},{2,226},{3,227},{4,228},{5,229},{6,230},{7,231},{8... | collective-permute-start | bytes 1179656 | tf_op jit(solution)/shard_map/ppermute | solution.py:324
  37.9 14.8 %collective-permute-start.2 = (bf16[512,384]{1,0:T(8,128)(2,1)S(1)}, bf16[512,384]{1,0:T(8,128)(2,1)S(1)}, u32[]{:S(2)}, u32[]{:S(2)}) collective-permute-start(bf16[512,384]{1,0:T(8,128)(2,1)S(1)} %collective-permute-done.1.refs_1_), channel_id=1, source_target_pairs={{0,32},{1,33},{2,34},{3,35},{4,36},{5,37},{6,38},{7,39},{8,40},{9,... | collective-permute-start | bytes 1179656 | tf_op jit(solution)/shard_map/ppermute | solution.py:323
  39.8 14.8 %collective-permute-start.5 = (bf16[512,384]{1,0:T(8,128)(2,1)S(1)}, bf16[512,384]{1,0:T(8,128)(2,1)S(1)}, u32[]{:S(2)}, u32[]{:S(2)}) collective-permute-start(bf16[512,384]{1,0:T(8,128)(2,1)S(1)} %collective-permute-done.3.refs_2_), channel_id=1, source_target_pairs={{0,224},{1,225},{2,226},{3,227},{4,228},{5,229},{6,230},{7,231},{8... | collective-permute-start | bytes 1179656 | tf_op jit(solution)/shard_map/ppermute | solution.py:324
  45.6 2.2 %copy-start.1 = (bf16[512,4096]{1,0:T(8,128)(2,1)S(1)}, bf16[512,4096]{1,0:T(8,128)(2,1)}, u32[]{:S(2)}) copy-start(bf16[512,4096]{1,0:T(8,128)(2,1)} %mine) | copy-start | bytes 12582916
  52.7 14.2 %collective-permute-start.4 = (bf16[512,384]{1,0:T(8,128)(2,1)S(1)}, bf16[512,384]{1,0:T(8,128)(2,1)S(1)}, u32[]{:S(2)}, u32[]{:S(2)}) collective-permute-start(bf16[512,384]{1,0:T(8,128)(2,1)S(1)} %collective-permute-done.2.refs_3_), channel_id=1, source_target_pairs={{0,32},{1,33},{2,34},{3,35},{4,36},{5,37},{6,38},{7,39},{8,40},{9,... | collective-permute-start | bytes 1179656 | tf_op jit(solution)/shard_map/ppermute | solution.py:323
  54.6 15.6 %collective-permute-start.7 = (bf16[512,384]{1,0:T(8,128)(2,1)S(1)}, bf16[512,384]{1,0:T(8,128)(2,1)S(1)}, u32[]{:S(2)}, u32[]{:S(2)}) collective-permute-start(bf16[512,384]{1,0:T(8,128)(2,1)S(1)} %collective-permute-done.5.refs_4_), channel_id=1, source_target_pairs={{0,224},{1,225},{2,226},{3,227},{4,228},{5,229},{6,230},{7,231},{8... | collective-permute-start | bytes 1179656 | tf_op jit(solution)/shard_map/ppermute | solution.py:324
  66.9 10.9 %collective-permute-start.6 = (bf16[512,384]{1,0:T(8,128)(2,1)S(1)}, bf16[512,384]{1,0:T(8,128)(2,1)S(1)}, u32[]{:S(2)}, u32[]{:S(2)}) collective-permute-start(bf16[512,384]{1,0:T(8,128)(2,1)S(1)} %collective-permute-done.4.refs_0_), channel_id=1, source_target_pairs={{0,32},{1,33},{2,34},{3,35},{4,36},{5,37},{6,38},{7,39},{8,40},{9,... | collective-permute-start | bytes 1179656 | tf_op jit(solution)/shard_map/ppermute | solution.py:323
  80.5 3.6 %collective-permute-start.8 = (bf16[512,384]{1,0:T(8,128)(2,1)S(1)}, bf16[512,384]{1,0:T(8,128)(2,1)S(1)}, u32[]{:S(2)}, u32[]{:S(2)}) collective-permute-start(bf16[512,384]{1,0:T(8,128)(2,1)S(1)} %get-tuple-element.37), channel_id=1, source_target_pairs={{0,256},{256,0},{1,257},{257,1},{2,258},{258,2},{3,259},{259,3},{4... | collective-permute-start | bytes 1179656 | tf_op jit(solution)/shard_map/ppermute | solution.py:38
  84.2 22.7 %collective-permute-start.9 = (bf16[512,256]{1,0:T(8,128)(2,1)S(1)}, bf16[512,256]{1,0:T(8,128)(2,1)S(1)}, u32[]{:S(2)}, u32[]{:S(2)}) collective-permute-start(bf16[512,256]{1,0:T(8,128)(2,1)S(1)} %pad_maximum_fusion.2.own), channel_id=1, source_target_pairs={{0,8},{1,9},{2,10},{3,11},{4,12},{5,13},{6,14},{7,15},{8,16},{9,17... | collective-permute-start | bytes 786440 | tf_op jit(solution)/shard_map/ppermute | solution.py:353
  88.5 20.4 %collective-permute-start.11 = (bf16[512,256]{1,0:T(8,128)(2,1)S(1)}, bf16[512,256]{1,0:T(8,128)(2,1)S(1)}, u32[]{:S(2)}, u32[]{:S(2)}) collective-permute-start(bf16[512,256]{1,0:T(8,128)(2,1)S(1)} %pad_maximum_fusion.2.own), channel_id=1, source_target_pairs={{0,24},{1,25},{2,26},{3,27},{4,28},{5,29},{6,30},{7,31},{8,32},{9,... | collective-permute-start | bytes 786440 | tf_op jit(solution)/shard_map/ppermute | solution.py:354
  106.8 12.5 %collective-permute-start.10 = (bf16[512,256]{1,0:T(8,128)(2,1)S(1)}, bf16[512,256]{1,0:T(8,128)(2,1)S(1)}, u32[]{:S(2)}, u32[]{:S(2)}) collective-permute-start(bf16[512,256]{1,0:T(8,128)(2,1)S(1)} %collective-permute-done.9.one_three), channel_id=1, source_target_pairs={{0,8},{1,9},{2,10},{3,11},{4,12},{5,13},{6,14},{7,15},{8,16},{9,17... | collective-permute-start | bytes 786440 | tf_op jit(solution)/shard_map/ppermute | solution.py:355

commit v3 on v2

--- a/solution.py
+++ b/solution.py
@@ -330,12 +330,11 @@
     (total,) = project_part(order, blocks, [(tokens, [0, 1, 2], None)], "first")
     ahead2, total = lax.optimization_barrier((ahead2, total))
     ahead3, back3 = send_ahead(ahead2), send_back(back2)
+    far = lax.ppermute(ahead2, axes, ring_pairs(lambda dp: 2 - 4 * dp))
     blocks += [ahead2, back2]
     totals = project_part(
         order, blocks, [(tokens, [3, 4], total), (tokens_other, [0, 1, 2, 3, 4], None)], "second"
     )
-    ahead3, *totals = lax.optimization_barrier((ahead3, *totals))
-    far = send_ahead(ahead3)
     totals = project_part(
         order[5:7],
         [ahead3, back3],

time: 124 us -> 122 us (0.984)
  the two profiles are of different devices: /device:TPU:260 before, /device:TPU:2 now
where the time goes in v3:
time: 122 us; the launch traced here: 121 us
  starting transfers between devices  50.9 us (42%)
  waiting for transfers between devices  39.6 us (32%)
  Pallas kernels  21.5 us (18%)
  local copies, waits for them, and re-layouts  5.44 us (4%)
  other arithmetic  3.6 us (3%)
    ppermute x3, starting transfers between devices, per_device(): send_back = lambda value: lax.ppermute(value, axes, back)  19.6 us
    ppermute x1, waiting for transfers between devices, per_device(): one_three = lax.ppermute(own, axes, shift_pairs(lambda dp: 1 + 2 * dp))  10.6 us
    all_to_all x1, waiting for transfers between devices, spread(): parts = lax.all_to_all(copies, axis, 0, 0)  10.6 us
    pallas_call x3, Pallas kernels, project_part(): pl.pallas_call(functools.partial(part_kernel, plan=[(use, carried is not...  9.54 us
    ppermute x3, starting transfers between devices, per_device(): send_ahead = lambda value: lax.ppermute(value, axes, ahead)  8.11 us
    all_to_all x1, starting transfers between devices, spread(): parts = lax.all_to_all(copies, axis, 0, 0)  7.09 us
    ppermute x1, waiting for transfers between devices, per_device(): two = lax.ppermute(one_three, axes, shift_pairs(lambda dp: 1 - 2 * dp))  6.39 us
    pallas_call x1, Pallas kernels, attend(): pl.pallas_call(near_kernel, grid_spec=pltpu.PrefetchScalarGridSpec(num_sc...  4.83 us
  transfers between devices with their start and end apart: 13, of which 8 were waited for; matrix products, arithmetic and copies ran while one was open for 4% of the time, Pallas kernels for 12%

profile of v3, /device:TPU:2, one launch (start us, length us, event | category | flops | bytes accessed | tf_op | source)
XLA Modules:
  0.0 121.3 jit_solution(8604186691051740259)
XLA Ops:
  0.0 0.0 copy-start
  0.0 0.9 copy-done
  0.9 0.8 dynamic-slice_bitcast_fusion.1
  1.7 0.8 broadcast_in_dim.22
  2.5 7.1 %all-to-all-start = ((bf16[4,128,384]{2,1,0:T(8,128)(2,1)}), bf16[4,128,384]{2,1,0:T(8,128)(2,1)S(1)}, u32[]{:S(2)}, u32[]{:S(2)}) async-start(bf16[4,128,384]{2,1,0:T(8,128)(2,1)} %broadcast_in_dim.22), calls=%async_computation | async-start | bytes 786432 | tf_op jit(solution)/shard_map/all_to_all | solution.py:43
  9.6 1.0 fusion
  10.6 0.8 select_reduce_fusion.1
  11.4 0.1 select_reduce_fusion
  11.5 0.1 pad_maximum_fusion.cosine
  11.6 0.1 pad_maximum_fusion.1.sine
  11.8 10.6 %all-to-all-done = bf16[4,128,384]{2,1,0:T(8,128)(2,1)S(1)} async-done(((bf16[4,128,384]{2,1,0:T(8,128)(2,1)}), bf16[4,128,384]{2,1,0:T(8,128)(2,1)S(1)}, u32[]{:S(2)}, u32[]{:S(2)}) %all-to-all-start) | async-done | bytes 393248 | tf_op jit(solution)/shard_map/all_to_all | solution.py:43
  22.4 1.9 %collective-permute-start = (bf16[512,4096]{1,0:T(8,128)(2,1)}, bf16[512,4096]{1,0:T(8,128)(2,1)}, u32[]{:S(2)}, u32[]{:S(2)}) collective-permute-start(bf16[512,4096]{1,0:T(8,128)(2,1)} %mine), channel_id=1, source_target_pairs={{0,256},{256,0},{1,257},{257,1},{2,258},{258,2},{3,259},{259,3},{4... | collective-permute-start | bytes 12582920 | tf_op jit(solution)/shard_map/ppermute | solution.py:38
  24.3 4.3 %collective-permute-start.1 = (bf16[512,384]{1,0:T(8,128)(2,1)S(1)}, bf16[512,384]{1,0:T(8,128)(2,1)S(1)}, u32[]{:S(2)}, u32[]{:S(2)}) collective-permute-start(bf16[512,384]{1,0:T(8,128)(2,1)S(1)} %bitcast.8), channel_id=1, source_target_pairs={{0,32},{1,33},{2,34},{3,35},{4,36},{5,37},{6,38},{7,39},{8,40},{9,... | collective-permute-start | bytes 1179656 | tf_op jit(solution)/shard_map/ppermute | solution.py:323
  28.6 8.6 %collective-permute-start.3 = (bf16[512,384]{1,0:T(8,128)(2,1)S(1)}, bf16[512,384]{1,0:T(8,128)(2,1)S(1)}, u32[]{:S(2)}, u32[]{:S(2)}) collective-permute-start(bf16[512,384]{1,0:T(8,128)(2,1)S(1)} %bitcast.9), channel_id=1, source_target_pairs={{0,224},{1,225},{2,226},{3,227},{4,228},{5,229},{6,230},{7,231},{8... | collective-permute-start | bytes 1179656 | tf_op jit(solution)/shard_map/ppermute | solution.py:324
  37.2 3.8 %collective-permute-done.1.refs_1_ = bf16[512,384]{1,0:T(8,128)(2,1)S(1)} collective-permute-done((bf16[512,384]{1,0:T(8,128)(2,1)S(1)}, bf16[512,384]{1,0:T(8,128)(2,1)S(1)}, u32[]{:S(2)}, u32[]{:S(2)}) %collective-permute-start.1) | collective-permute-done | bytes 393248 | tf_op jit(solution)/shard_map/ppermute | solution.py:323
  41.0 1.9 %collective-permute-start.2 = (bf16[512,384]{1,0:T(8,128)(2,1)S(1)}, bf16[512,384]{1,0:T(8,128)(2,1)S(1)}, u32[]{:S(2)}, u32[]{:S(2)}) collective-permute-start(bf16[512,384]{1,0:T(8,128)(2,1)S(1)} %collective-permute-done.1.refs_1_), channel_id=1, source_target_pairs={{0,32},{1,33},{2,34},{3,35},{4,36},{5,37},{6,38},{7,39},{8,40},{9,... | collective-permute-start | bytes 1179656 | tf_op jit(solution)/shard_map/ppermute | solution.py:323
  42.9 1.4 %collective-permute-done.3.refs_2_ = bf16[512,384]{1,0:T(8,128)(2,1)S(1)} collective-permute-done((bf16[512,384]{1,0:T(8,128)(2,1)S(1)}, bf16[512,384]{1,0:T(8,128)(2,1)S(1)}, u32[]{:S(2)}, u32[]{:S(2)}) %collective-permute-start.3) | collective-permute-done | bytes 393248 | tf_op jit(solution)/shard_map/ppermute | solution.py:324
  44.2 5.6 %collective-permute-start.6 = (bf16[512,384]{1,0:T(8,128)(2,1)S(1)}, bf16[512,384]{1,0:T(8,128)(2,1)S(1)}, u32[]{:S(2)}, u32[]{:S(2)}) collective-permute-start(bf16[512,384]{1,0:T(8,128)(2,1)S(1)} %collective-permute-done.3.refs_2_), channel_id=1, source_target_pairs={{0,224},{1,225},{2,226},{3,227},{4,228},{5,229},{6,230},{7,231},{8... | collective-permute-start | bytes 1179656 | tf_op jit(solution)/shard_map/ppermute | solution.py:324
  49.8 0.7 and_select_fusion.order
  50.5 0.0 copy-start.1
  50.5 2.2 %copy-done.1 = bf16[512,4096]{1,0:T(8,128)(2,1)S(1)} copy-done((bf16[512,4096]{1,0:T(8,128)(2,1)S(1)}, bf16[512,4096]{1,0:T(8,128)(2,1)}, u32[]{:S(2)}) %copy-start.1) | copy-done | bytes 4194328
  52.7 1.9 %first.1.refs_7_ = f32[512,384]{1,0:T(8,128)S(1)} custom-call(s32[8]{0:T(128)S(1)} %and_select_fusion.order, bf16[512,384]{1,0:T(8,128)(2,1)S(1)} %bitcast.10, bf16[512,384]{1,0:T(8,128)(2,1)S(1)} %collective-permute-done.1.refs_1_, bf16[512,384]{1,0:T(8,128)(2,1)S(1)} %collective-permute-done.3.refs_2_, bf16[512,4096]{1,0:T(8,128)(2,1)S(1)} %copy-done.1, ...), custom_call_target="tpu_custom_call" | custom-call | flops 603979776 | bytes 2359296 | tf_op jit(solution)/shard_map/first/pallas_call | solution.py:76
  54.6 0.0 collective-permute-done.2.refs_3_
  54.6 1.9 %collective-permute-start.5 = (bf16[512,384]{1,0:T(8,128)(2,1)S(1)}, bf16[512,384]{1,0:T(8,128)(2,1)S(1)}, u32[]{:S(2)}, u32[]{:S(2)}) collective-permute-start(bf16[512,384]{1,0:T(8,128)(2,1)S(1)} %collective-permute-done.2.refs_3_), channel_id=1, source_target_pairs={{0,32},{1,33},{2,34},{3,35},{4,36},{5,37},{6,38},{7,39},{8,40},{9,... | collective-permute-start | bytes 1179656 | tf_op jit(solution)/shard_map/ppermute | solution.py:323
  56.5 0.0 collective-permute-done.6.refs_4_
  56.5 5.4 %collective-permute-start.7 = (bf16[512,384]{1,0:T(8,128)(2,1)S(1)}, bf16[512,384]{1,0:T(8,128)(2,1)S(1)}, u32[]{:S(2)}, u32[]{:S(2)}) collective-permute-start(bf16[512,384]{1,0:T(8,128)(2,1)S(1)} %collective-permute-done.6.refs_4_), channel_id=1, source_target_pairs={{0,224},{1,225},{2,226},{3,227},{4,228},{5,229},{6,230},{7,231},{8... | collective-permute-start | bytes 1179656 | tf_op jit(solution)/shard_map/ppermute | solution.py:324
  62.0 2.9 %collective-permute-start.4 = (bf16[512,384]{1,0:T(8,128)(2,1)S(1)}, bf16[512,384]{1,0:T(8,128)(2,1)S(1)}, u32[]{:S(2)}, u32[]{:S(2)}) collective-permute-start(bf16[512,384]{1,0:T(8,128)(2,1)S(1)} %collective-permute-done.2.refs_3_), channel_id=1, source_target_pairs={{0,64},{1,65},{2,66},{3,67},{4,68},{5,69},{6,70},{7,71},{8,72},{9,... | collective-permute-start | bytes 1179656 | tf_op jit(solution)/shard_map/ppermute | solution.py:333
  64.9 0.1 slice.13.order
  64.9 0.6 slice.12
  65.5 0.7 pad_add_fusion.scalars
  66.2 0.0 collective-permute-done.refs_8_.refs_9_.refs_10_.refs_11_.refs_12_.refs_5_.refs_6_.other
  66.2 4.4 %second.1 = (f32[512,384]{1,0:T(8,128)S(1)}, f32[512,384]{1,0:T(8,128)S(1)}) custom-call(s32[8]{0:T(128)S(1)} %and_select_fusion.order, bf16[512,384]{1,0:T(8,128)(2,1)S(1)} %bitcast.11, bf16[512,384]{1,0:T(8,128)(2,1)S(1)} %collective-permute-done.1.refs_1_, bf16[512,384]{1,0:T(8,128)(2,1)S(1)} %collective-permute-done.3.refs_2_, ...), custom_call_target="tpu_custom_call" | custom-call | flops 1409286144 | bytes 5505024 | tf_op jit(solution)/shard_map/second/pallas_call | solution.py:76
  70.7 0.0 collective-permute-done.5.refs_0_
  70.7 3.1 %collective-permute-done.7.refs_1_ = bf16[512,384]{1,0:T(8,128)(2,1)S(1)} collective-permute-done((bf16[512,384]{1,0:T(8,128)(2,1)S(1)}, bf16[512,384]{1,0:T(8,128)(2,1)S(1)}, u32[]{:S(2)}, u32[]{:S(2)}) %collective-permute-start.7) | collective-permute-done | bytes 393248 | tf_op jit(solution)/shard_map/ppermute | solution.py:324
  73.8 3.2 %third.1 = (f32[512,384]{1,0:T(8,128)S(1)}, f32[512,384]{1,0:T(8,128)S(1)}) custom-call(s32[2]{0:T(128)S(1)} %slice.13.order, bf16[512,384]{1,0:T(8,128)(2,1)S(1)} %collective-permute-done.5.refs_0_, bf16[512,384]{1,0:T(8,128)(2,1)S(1)} %collective-permute-done.7.refs_1_, bf16[512,4096]{1,0:T(8,128)(2,1)} %mine, bf16[512,4096]{1,0:T(8,128)(2,1)} %mine, ...), custom_call_target="tpu_custom_call" | custom-call | flops 805306368 | bytes 3145728 | tf_op jit(solution)/shard_map/third/pallas_call | solution.py:76
  77.1 2.0 %collective-permute-done.4.weight = bf16[512,384]{1,0:T(8,128)(2,1)S(1)} collective-permute-done((bf16[512,384]{1,0:T(8,128)(2,1)S(1)}, bf16[512,384]{1,0:T(8,128)(2,1)S(1)}, u32[]{:S(2)}, u32[]{:S(2)}) %collective-permute-start.4) | collective-permute-done | bytes 393248 | tf_op jit(solution)/shard_map/ppermute | solution.py:333
  79.1 2.7 %finish.1 = (bf16[512,384]{1,0:T(8,128)(2,1)S(1)}, bf16[512,384]{1,0:T(8,128)(2,1)S(1)}) custom-call(s32[2]{0:T(128)S(1)} %pad_add_fusion.scalars, bf16[512,4096]{1,0:T(8,128)(2,1)} %mine, bf16[512,4096]{1,0:T(8,128)(2,1)} %collective-permute-done.refs_8_.refs_9_.refs_10_.refs_11_.refs_12_.refs_5_.refs_6_.other, ...), custom_call_target="tpu_custom_call" | custom-call | flops 402653184 | bytes 2621440 | tf_op jit(solution)/shard_map/finish/pallas_call | solution.py:120
  81.8 1.9 %collective-permute-start.8 = (bf16[512,384]{1,0:T(8,128)(2,1)S(1)}, bf16[512,384]{1,0:T(8,128)(2,1)S(1)}, u32[]{:S(2)}, u32[]{:S(2)}) collective-permute-start(bf16[512,384]{1,0:T(8,128)(2,1)S(1)} %get-tuple-element.31), channel_id=1, source_target_pairs={{0,256},{256,0},{1,257},{257,1},{2,258},{258,2},{3,259},{259,3},{4... | collective-permute-start | bytes 1179656 | tf_op jit(solution)/shard_map/ppermute | solution.py:38
  83.7 1.7 %collective-permute-done.8.q_other = bf16[512,384]{1,0:T(8,128)(2,1)S(1)} collective-permute-done((bf16[512,384]{1,0:T(8,128)(2,1)S(1)}, bf16[512,384]{1,0:T(8,128)(2,1)S(1)}, u32[]{:S(2)}, u32[]{:S(2)}) %collective-permute-start.8) | collective-permute-done | bytes 393248 | tf_op jit(solution)/shard_map/ppermute | solution.py:38
  85.5 4.4 %collective-permute-start.9 = (bf16[512,256]{1,0:T(8,128)(2,1)S(1)}, bf16[512,256]{1,0:T(8,128)(2,1)S(1)}, u32[]{:S(2)}, u32[]{:S(2)}) collective-permute-start(bf16[512,256]{1,0:T(8,128)(2,1)S(1)} %pad_maximum_fusion.2.own), channel_id=1, source_target_pairs={{0,8},{1,9},{2,10},{3,11},{4,12},{5,13},{6,14},{7,15},{8,16},{9,17... | collective-permute-start | bytes 786440 | tf_op jit(solution)/shard_map/ppermute | solution.py:352
  89.8 3.1 %collective-permute-start.11 = (bf16[512,256]{1,0:T(8,128)(2,1)S(1)}, bf16[512,256]{1,0:T(8,128)(2,1)S(1)}, u32[]{:S(2)}, u32[]{:S(2)}) collective-permute-start(bf16[512,256]{1,0:T(8,128)(2,1)S(1)} %pad_maximum_fusion.2.own), channel_id=1, source_target_pairs={{0,24},{1,25},{2,26},{3,27},{4,28},{5,29},{6,30},{7,31},{8,32},{9,... | collective-permute-start | bytes 786440 | tf_op jit(solution)/shard_map/ppermute | solution.py:353
  92.9 10.6 %collective-permute-done.9.one_three = bf16[512,256]{1,0:T(8,128)(2,1)S(1)} collective-permute-done((bf16[512,256]{1,0:T(8,128)(2,1)S(1)}, bf16[512,256]{1,0:T(8,128)(2,1)S(1)}, u32[]{:S(2)}, u32[]{:S(2)}) %collective-permute-start.9) | collective-permute-done | bytes 262176 | tf_op jit(solution)/shard_map/ppermute | solution.py:352
  103.6 1.9 %collective-permute-start.10 = (bf16[512,256]{1,0:T(8,128)(2,1)S(1)}, bf16[512,256]{1,0:T(8,128)(2,1)S(1)}, u32[]{:S(2)}, u32[]{:S(2)}) collective-permute-start(bf16[512,256]{1,0:T(8,128)(2,1)S(1)} %collective-permute-done.9.one_three), channel_id=1, source_target_pairs={{0,8},{1,9},{2,10},{3,11},{4,12},{5,13},{6,14},{7,15},{8,16},{9,17... | collective-permute-start | bytes 786440 | tf_op jit(solution)/shard_map/ppermute | solution.py:354
  105.5 0.1 copy.9.starts
  105.6 0.0 collective-permute-done.11.three_one
  105.6 4.8 %attend_near.1 = (f32[2048,128]{1,0:T(8,128)S(1)}, f32[2048,128]{1,0:T(8,128)S(1)}) custom-call(s32[1]{0:T(128)} %bitcast.core, bf16[512,384]{1,0:T(8,128)(2,1)S(1)} %get-tuple-element.30.q_mine, bf16[512,384]{1,0:T(8,128)(2,1)S(1)} %collective-permute-done.8.q_other, bf16[512,256]{1,0:T(8,128)(2,1)S(1)} %collective-permute-done.9.one_three, ...), custom_call_target="tpu_custom_call" | custom-call | flops 1207959552 | bytes 2097152 | tf_op jit(solution)/shard_map/attend_near/pallas_call | solution.py:251
  110.5 6.4 %collective-permute-done.10.two = bf16[512,256]{1,0:T(8,128)(2,1)S(1)} collective-permute-done((bf16[512,256]{1,0:T(8,128)(2,1)S(1)}, bf16[512,256]{1,0:T(8,128)(2,1)S(1)}, u32[]{:S(2)}, u32[]{:S(2)}) %collective-permute-start.10) | collective-permute-done | bytes 262176 | tf_op jit(solution)/shard_map/ppermute | solution.py:354
  116.9 4.4 %attend_last.1 = bf16[512,512]{1,0:T(8,128)(2,1)} custom-call(s32[1]{0:T(128)} %bitcast.core, bf16[512,384]{1,0:T(8,128)(2,1)S(1)} %get-tuple-element.30.q_mine, bf16[512,384]{1,0:T(8,128)(2,1)S(1)} %collective-permute-done.8.q_other, bf16[512,256]{1,0:T(8,128)(2,1)S(1)} %collective-permute-done.10.two, s32[512,1]{1,0:T(8,128)S(1)} %copy.9.starts, ...), custom_call_target="tpu_custom_call" | custom-call | flops 536870912 | bytes 2097152 | tf_op jit(solution)/shard_map/attend_last/pallas_call | solution.py:270
  (7 shorter events, 0.1 us)
Async XLA Ops:
  0.0 0.9 copy-start
  2.5 19.9 %all-to-all-start = ((bf16[4,128,384]{2,1,0:T(8,128)(2,1)}), bf16[4,128,384]{2,1,0:T(8,128)(2,1)S(1)}, u32[]{:S(2)}, u32[]{:S(2)}) async-start(bf16[4,128,384]{2,1,0:T(8,128)(2,1)} %broadcast_in_dim.22), calls=%async_computation | async-start | bytes 786432 | tf_op jit(solution)/shard_map/all_to_all | solution.py:43
  22.4 43.9 %collective-permute-start = (bf16[512,4096]{1,0:T(8,128)(2,1)}, bf16[512,4096]{1,0:T(8,128)(2,1)}, u32[]{:S(2)}, u32[]{:S(2)}) collective-permute-start(bf16[512,4096]{1,0:T(8,128)(2,1)} %mine), channel_id=1, source_target_pairs={{0,256},{256,0},{1,257},{257,1},{2,258},{258,2},{3,259},{259,3},{4... | collective-permute-start | bytes 12582920 | tf_op jit(solution)/shard_map/ppermute | solution.py:38
  24.3 16.7 %collective-permute-start.1 = (bf16[512,384]{1,0:T(8,128)(2,1)S(1)}, bf16[512,384]{1,0:T(8,128)(2,1)S(1)}, u32[]{:S(2)}, u32[]{:S(2)}) collective-permute-start(bf16[512,384]{1,0:T(8,128)(2,1)S(1)} %bitcast.8), channel_id=1, source_target_pairs={{0,32},{1,33},{2,34},{3,35},{4,36},{5,37},{6,38},{7,39},{8,40},{9,... | collective-permute-start | bytes 1179656 | tf_op jit(solution)/shard_map/ppermute | solution.py:323
  28.6 15.7 %collective-permute-start.3 = (bf16[512,384]{1,0:T(8,128)(2,1)S(1)}, bf16[512,384]{1,0:T(8,128)(2,1)S(1)}, u32[]{:S(2)}, u32[]{:S(2)}) collective-permute-start(bf16[512,384]{1,0:T(8,128)(2,1)S(1)} %bitcast.9), channel_id=1, source_target_pairs={{0,224},{1,225},{2,226},{3,227},{4,228},{5,229},{6,230},{7,231},{8... | collective-permute-start | bytes 1179656 | tf_op jit(solution)/shard_map/ppermute | solution.py:324
  41.0 13.6 %collective-permute-start.2 = (bf16[512,384]{1,0:T(8,128)(2,1)S(1)}, bf16[512,384]{1,0:T(8,128)(2,1)S(1)}, u32[]{:S(2)}, u32[]{:S(2)}) collective-permute-start(bf16[512,384]{1,0:T(8,128)(2,1)S(1)} %collective-permute-done.1.refs_1_), channel_id=1, source_target_pairs={{0,32},{1,33},{2,34},{3,35},{4,36},{5,37},{6,38},{7,39},{8,40},{9,... | collective-permute-start | bytes 1179656 | tf_op jit(solution)/shard_map/ppermute | solution.py:323
  44.2 12.3 %collective-permute-start.6 = (bf16[512,384]{1,0:T(8,128)(2,1)S(1)}, bf16[512,384]{1,0:T(8,128)(2,1)S(1)}, u32[]{:S(2)}, u32[]{:S(2)}) collective-permute-start(bf16[512,384]{1,0:T(8,128)(2,1)S(1)} %collective-permute-done.3.refs_2_), channel_id=1, source_target_pairs={{0,224},{1,225},{2,226},{3,227},{4,228},{5,229},{6,230},{7,231},{8... | collective-permute-start | bytes 1179656 | tf_op jit(solution)/shard_map/ppermute | solution.py:324
  50.5 2.2 %copy-start.1 = (bf16[512,4096]{1,0:T(8,128)(2,1)S(1)}, bf16[512,4096]{1,0:T(8,128)(2,1)}, u32[]{:S(2)}) copy-start(bf16[512,4096]{1,0:T(8,128)(2,1)} %mine) | copy-start | bytes 12582916
  54.6 16.1 %collective-permute-start.5 = (bf16[512,384]{1,0:T(8,128)(2,1)S(1)}, bf16[512,384]{1,0:T(8,128)(2,1)S(1)}, u32[]{:S(2)}, u32[]{:S(2)}) collective-permute-start(bf16[512,384]{1,0:T(8,128)(2,1)S(1)} %collective-permute-done.2.refs_3_), channel_id=1, source_target_pairs={{0,32},{1,33},{2,34},{3,35},{4,36},{5,37},{6,38},{7,39},{8,40},{9,... | collective-permute-start | bytes 1179656 | tf_op jit(solution)/shard_map/ppermute | solution.py:323
  56.5 17.3 %collective-permute-start.7 = (bf16[512,384]{1,0:T(8,128)(2,1)S(1)}, bf16[512,384]{1,0:T(8,128)(2,1)S(1)}, u32[]{:S(2)}, u32[]{:S(2)}) collective-permute-start(bf16[512,384]{1,0:T(8,128)(2,1)S(1)} %collective-permute-done.6.refs_4_), channel_id=1, source_target_pairs={{0,224},{1,225},{2,226},{3,227},{4,228},{5,229},{6,230},{7,231},{8... | collective-permute-start | bytes 1179656 | tf_op jit(solution)/shard_map/ppermute | solution.py:324
  62.0 17.1 %collective-permute-start.4 = (bf16[512,384]{1,0:T(8,128)(2,1)S(1)}, bf16[512,384]{1,0:T(8,128)(2,1)S(1)}, u32[]{:S(2)}, u32[]{:S(2)}) collective-permute-start(bf16[512,384]{1,0:T(8,128)(2,1)S(1)} %collective-permute-done.2.refs_3_), channel_id=1, source_target_pairs={{0,64},{1,65},{2,66},{3,67},{4,68},{5,69},{6,70},{7,71},{8,72},{9,... | collective-permute-start | bytes 1179656 | tf_op jit(solution)/shard_map/ppermute | solution.py:333
  81.8 3.6 %collective-permute-start.8 = (bf16[512,384]{1,0:T(8,128)(2,1)S(1)}, bf16[512,384]{1,0:T(8,128)(2,1)S(1)}, u32[]{:S(2)}, u32[]{:S(2)}) collective-permute-start(bf16[512,384]{1,0:T(8,128)(2,1)S(1)} %get-tuple-element.31), channel_id=1, source_target_pairs={{0,256},{256,0},{1,257},{257,1},{2,258},{258,2},{3,259},{259,3},{4... | collective-permute-start | bytes 1179656 | tf_op jit(solution)/shard_map/ppermute | solution.py:38
  85.5 18.1 %collective-permute-start.9 = (bf16[512,256]{1,0:T(8,128)(2,1)S(1)}, bf16[512,256]{1,0:T(8,128)(2,1)S(1)}, u32[]{:S(2)}, u32[]{:S(2)}) collective-permute-start(bf16[512,256]{1,0:T(8,128)(2,1)S(1)} %pad_maximum_fusion.2.own), channel_id=1, source_target_pairs={{0,8},{1,9},{2,10},{3,11},{4,12},{5,13},{6,14},{7,15},{8,16},{9,17... | collective-permute-start | bytes 786440 | tf_op jit(solution)/shard_map/ppermute | solution.py:352
  89.8 15.8 %collective-permute-start.11 = (bf16[512,256]{1,0:T(8,128)(2,1)S(1)}, bf16[512,256]{1,0:T(8,128)(2,1)S(1)}, u32[]{:S(2)}, u32[]{:S(2)}) collective-permute-start(bf16[512,256]{1,0:T(8,128)(2,1)S(1)} %pad_maximum_fusion.2.own), channel_id=1, source_target_pairs={{0,24},{1,25},{2,26},{3,27},{4,28},{5,29},{6,30},{7,31},{8,32},{9,... | collective-permute-start | bytes 786440 | tf_op jit(solution)/shard_map/ppermute | solution.py:353
  103.6 13.3 %collective-permute-start.10 = (bf16[512,256]{1,0:T(8,128)(2,1)S(1)}, bf16[512,256]{1,0:T(8,128)(2,1)S(1)}, u32[]{:S(2)}, u32[]{:S(2)}) collective-permute-start(bf16[512,256]{1,0:T(8,128)(2,1)S(1)} %collective-permute-done.9.one_three), channel_id=1, source_target_pairs={{0,8},{1,9},{2,10},{3,11},{4,12},{5,13},{6,14},{7,15},{8,16},{9,17... | collective-permute-start | bytes 786440 | tf_op jit(solution)/shard_map/ppermute | solution.py:354

commit v4 on v3

--- a/solution.py
+++ b/solution.py
@@ -111,7 +111,7 @@
 
 def finish(scalars, mine, other, weight, totals, cosine, sine):
     rows, (depth, columns) = mine.shape[0], weight.shape
-    steps = 2
+    steps = 1
     part = rows // steps
     head_dim = cosine.shape[1]
     tokens = pl.BlockSpec((part, depth), lambda i, scalars: (i, scalars[0]))
@@ -176,88 +176,85 @@
     return total, result
 
 
-def tile_inputs(half, q_mine, q_other, starts, first, head_dim):
+def tile_inputs(queries, starts, first, heads, head_dim):
     here = slice(first, first + tile)
-    queries = jnp.where(half == 0, q_mine[here], q_other[here])
-    heads = queries.shape[1] // head_dim
-    queries = jnp.concatenate(
-        [queries[:, h * head_dim : (h + 1) * head_dim] for h in range(heads)], axis=0
-    )
-    return queries, jnp.concatenate([starts[here]] * heads, axis=0)
-
-
-def near_kernel(core, q_mine, q_other, one_three, three_one, own, starts, partial, stats, three, one):
-    half = pl.program_id(0)
-
-    @pl.when((half == 0) & (core[0] == 0))
+    stacked = jnp.concatenate(
+        [queries[here, h * head_dim : (h + 1) * head_dim] for h in range(heads)], axis=0
+    )
+    return stacked, jnp.concatenate([starts[here]] * heads, axis=0)
+
+
+def near_kernel(
+    core, q_mine, q_other, one_three, three_one, own, starts, partial, stats, three, one, *, heads
+):
+    rows, head_dim = own.shape[0], own.shape[1] // 2
+
+    @pl.when(core[0] == 0)
     def _():
         one[...] = one_three[...]
         three[...] = three_one[...]
 
-    @pl.when((half == 0) & (core[0] == 1))
+    @pl.when(core[0] == 1)
     def _():
         three[...] = one_three[...]
         one[...] = three_one[...]
 
+    height = heads * tile
+    for half, q in enumerate((q_mine, q_other)):
+        for first in range(0, rows, tile):
+            queries, start = tile_inputs(q, starts, first, heads, head_dim)
+            pieces = [
+                (three, first, rows, 0),
+                (one, 0, rows, 2 * rows),
+                (own, 0, first + tile, 3 * rows),
+            ]
+            scores = score_pieces(queries, start, pieces, first)
+            peak = functools.reduce(
+                jnp.maximum, [jnp.max(part, axis=1, keepdims=True) for part in scores]
+            )
+            total, result = gather_pieces(scores, pieces, peak)
+            base = (half * rows + first) * heads
+            place = slice(base, base + height)
+            partial[place] = result
+            lane = lax.broadcasted_iota(jnp.int32, (height, head_dim), 1)
+            stats[place] = jnp.where(lane < head_dim // 2, peak, total)
+
+
+def last_kernel(core, q_mine, q_other, two, starts, partial, stats, out, *, heads):
+    rows, head_dim = two.shape[0], two.shape[1] // 2
+    height = heads * tile
+    for half, q in enumerate((q_mine, q_other)):
+        for first in range(0, rows, tile):
+            queries, start = tile_inputs(q, starts, first, heads, head_dim)
+            pieces = [(two, 0, rows, rows)]
+            scores = score_pieces(queries, start, pieces, first)
+            base = (half * rows + first) * heads
+            place = slice(base, base + height)
+            peak = stats[place, 0:1]
+            total = stats[place, head_dim // 2 : head_dim // 2 + 1]
+            top = jnp.maximum(peak, jnp.max(scores[0], axis=1, keepdims=True))
+            more, result = gather_pieces(scores, pieces, top)
+            keep = jnp.exp2(peak - top)
+            result = ((partial[place] * keep + result) / (total * keep + more)).astype(out.dtype)
+            for h in range(heads):
+                column = ((half + core[0]) % 2 * heads + h) * head_dim
+                out[first : first + tile, pl.ds(pl.multiple_of(column, head_dim), head_dim)] = (
+                    result[h * tile : (h + 1) * tile]
+                )
+
+
+def attend(core, q_mine, q_other, columns, one_three, three_one, two, own, starts):
     rows, head_dim = own.shape[0], own.shape[1] // 2
-    for first in range(0, rows, tile):
-        queries, start = tile_inputs(half, q_mine, q_other, starts, first, head_dim)
-        pieces = [
-            (three, first, rows, 0),
-            (one, 0, rows, 2 * rows),
-            (own, 0, first + tile, 3 * rows),
-        ]
-        scores = score_pieces(queries, start, pieces, first)
-        peak = functools.reduce(
-            jnp.maximum, [jnp.max(part, axis=1, keepdims=True) for part in scores]
-        )
-        total, result = gather_pieces(scores, pieces, peak)
-        height = queries.shape[0]
-        place = slice(first // tile * height, (first // tile + 1) * height)
-        partial[place] = result
-        lane = lax.broadcasted_iota(jnp.int32, (height, head_dim), 1)
-        stats[place] = jnp.where(lane < head_dim // 2, peak, total)
-
-
-def last_kernel(core, q_mine, q_other, two, starts, partial, stats, out):
-    half = pl.program_id(0)
-    rows, head_dim = two.shape[0], two.shape[1] // 2
-    for first in range(0, rows, tile):
-        queries, start = tile_inputs(half, q_mine, q_other, starts, first, head_dim)
-        height = queries.shape[0]
-        pieces = [(two, 0, rows, rows)]
-        scores = score_pieces(queries, start, pieces, first)
-        place = slice(first // tile * height, (first // tile + 1) * height)
-        peak = stats[place, 0:1]
-        total = stats[place, head_dim // 2 : head_dim // 2 + 1]
-        top = jnp.maximum(peak, jnp.max(scores[0], axis=1, keepdims=True))
-        more, result = gather_pieces(scores, pieces, top)
-        keep = jnp.exp2(peak - top)
-        result = ((partial[place] * keep + result) / (total * keep + more)).astype(out.dtype)
-        for h in range(height // tile):
-            out[first : first + tile, h * head_dim : (h + 1) * head_dim] = result[
-                h * tile : (h + 1) * tile
-            ]
-
-
-def attend(core, q_mine, q_other, columns, one_three, three_one, two, own, starts):
-    rows = own.shape[0]
-    head_dim = own.shape[1] // 2
-    height = rows * columns // head_dim
-    whole = lambda array: pl.BlockSpec(array.shape, lambda i, core: (0, 0))
-    half = pl.BlockSpec((rows, columns), lambda i, core: (0, 0))
-    args = (q_mine, q_other, one_three, three_one, own, starts)
-    kept = pl.BlockSpec((height, head_dim), lambda i, core: (i, 0))
+    heads = columns // head_dim
+    scalar = pl.BlockSpec(memory_space=pltpu.SMEM)
+    vector = pl.BlockSpec(memory_space=pltpu.VMEM)
+    args = (core, q_mine, q_other, one_three, three_one, own, starts)
     partial, stats = pl.pallas_call(
-        near_kernel,
-        grid_spec=pltpu.PrefetchScalarGridSpec(
-            num_scalar_prefetch=1,
-            grid=(2,),
-            in_specs=[half, half] + [whole(array) for array in args[2:]],
-            out_specs=[kept, kept],
-            scratch_shapes=[pltpu.VMEM(own.shape, own.dtype)] * 2,
-        ),
-        out_shape=[jax.ShapeDtypeStruct((2 * height, head_dim), jnp.float32)] * 2,
+        functools.partial(near_kernel, heads=heads),
+        in_specs=[scalar] + [vector] * (len(args) - 1),
+        out_specs=[vector, vector],
+        scratch_shapes=[pltpu.VMEM(own.shape, own.dtype)] * 2,
+        out_shape=[jax.ShapeDtypeStruct((2 * heads * rows, head_dim), jnp.float32)] * 2,
         compiler_params=pltpu.CompilerParams(vmem_limit_bytes=vmem_bytes),
         cost_estimate=pl.CostEstimate(
             flops=8 * rows * 9 * tile * columns,
@@ -265,16 +262,12 @@
             transcendentals=4 * rows * 9 * tile,
         ),
         name="attend_near",
-    )(core, *args)
-    args = (q_mine, q_other, two, starts)
+    )(*args)
+    args = (core, q_mine, q_other, two, starts, partial, stats)
     return pl.pallas_call(
-        last_kernel,
-        grid_spec=pltpu.PrefetchScalarGridSpec(
-            num_scalar_prefetch=1,
-            grid=(2,),
-            in_specs=[half, half] + [whole(array) for array in args[2:]] + [kept, kept],
-            out_specs=pl.BlockSpec((rows, columns), lambda i, core: (0, (i + core[0]) % 2)),
-        ),
+        functools.partial(last_kernel, heads=heads),
+        in_specs=[scalar] + [vector] * (len(args) - 1),
+        out_specs=vector,
         out_shape=jax.ShapeDtypeStruct((rows, 2 * columns), jnp.bfloat16),
         compiler_params=pltpu.CompilerParams(vmem_limit_bytes=vmem_bytes),
         cost_estimate=pl.CostEstimate(
@@ -283,7 +276,7 @@
             transcendentals=4 * rows * 4 * tile,
         ),
         name="attend_last",
-    )(core, *args, partial, stats)
+    )(*args)
 
 
 def per_device(tokens, lengths, q_weight, kv_weight):

time: 122 us -> 122 us (level)
  no operation moved by 1% of the time
where the time goes in v4:
time: 122 us; the launch traced here: 121 us
  starting transfers between devices  50.9 us (42%)
  waiting for transfers between devices  39.7 us (33%)
  Pallas kernels  21.2 us (17%)
  local copies, waits for them, and re-layouts  5.44 us (4%)
  other arithmetic  3.6 us (3%)
    ppermute x3, starting transfers between devices, per_device(): send_back = lambda value: lax.ppermute(value, axes, back)  19.6 us
    ppermute x1, waiting for transfers between devices, per_device(): one_three = lax.ppermute(own, axes, shift_pairs(lambda dp: 1 + 2 * dp))  10.6 us
    all_to_all x1, waiting for transfers between devices, spread(): parts = lax.all_to_all(copies, axis, 0, 0)  10.6 us
    pallas_call x3, Pallas kernels, project_part(): pl.pallas_call(functools.partial(part_kernel, plan=[(use, carried is not...  9.55 us
    ppermute x3, starting transfers between devices, per_device(): send_ahead = lambda value: lax.ppermute(value, axes, ahead)  8.11 us
    all_to_all x1, starting transfers between devices, spread(): parts = lax.all_to_all(copies, axis, 0, 0)  7.09 us
    ppermute x1, waiting for transfers between devices, per_device(): two = lax.ppermute(one_three, axes, shift_pairs(lambda dp: 1 - 2 * dp))  6.45 us
    pallas_call x1, Pallas kernels, attend(): pl.pallas_call(functools.partial(near_kernel, heads=heads), in_specs=[sca...  4.79 us
  transfers between devices with their start and end apart: 13, of which 8 were waited for; matrix products, arithmetic and copies ran while one was open for 4% of the time, Pallas kernels for 12%

profile of v4, /device:TPU:2, one launch (start us, length us, event | category | flops | bytes accessed | tf_op | source)
XLA Modules:
  0.0 121.0 jit_solution(1622826760529617091)
XLA Ops:
  0.0 0.0 copy-start
  0.0 0.9 copy-done
  0.9 0.8 dynamic-slice_bitcast_fusion.1
  1.7 0.8 broadcast_in_dim.22
  2.5 7.1 %all-to-all-start = ((bf16[4,128,384]{2,1,0:T(8,128)(2,1)}), bf16[4,128,384]{2,1,0:T(8,128)(2,1)S(1)}, u32[]{:S(2)}, u32[]{:S(2)}) async-start(bf16[4,128,384]{2,1,0:T(8,128)(2,1)} %broadcast_in_dim.22), calls=%async_computation | async-start | bytes 786432 | tf_op jit(solution)/shard_map/all_to_all | solution.py:43
  9.6 1.0 fusion
  10.6 0.8 select_reduce_fusion.1
  11.4 0.1 select_reduce_fusion
  11.5 0.1 pad_maximum_fusion.cosine
  11.6 0.1 pad_maximum_fusion.1.sine
  11.8 10.6 %all-to-all-done = bf16[4,128,384]{2,1,0:T(8,128)(2,1)S(1)} async-done(((bf16[4,128,384]{2,1,0:T(8,128)(2,1)}), bf16[4,128,384]{2,1,0:T(8,128)(2,1)S(1)}, u32[]{:S(2)}, u32[]{:S(2)}) %all-to-all-start) | async-done | bytes 393248 | tf_op jit(solution)/shard_map/all_to_all | solution.py:43
  22.4 1.9 %collective-permute-start = (bf16[512,4096]{1,0:T(8,128)(2,1)}, bf16[512,4096]{1,0:T(8,128)(2,1)}, u32[]{:S(2)}, u32[]{:S(2)}) collective-permute-start(bf16[512,4096]{1,0:T(8,128)(2,1)} %mine), channel_id=1, source_target_pairs={{0,256},{256,0},{1,257},{257,1},{2,258},{258,2},{3,259},{259,3},{4... | collective-permute-start | bytes 12582920 | tf_op jit(solution)/shard_map/ppermute | solution.py:38
  24.3 4.3 %collective-permute-start.1 = (bf16[512,384]{1,0:T(8,128)(2,1)S(1)}, bf16[512,384]{1,0:T(8,128)(2,1)S(1)}, u32[]{:S(2)}, u32[]{:S(2)}) collective-permute-start(bf16[512,384]{1,0:T(8,128)(2,1)S(1)} %bitcast.8), channel_id=1, source_target_pairs={{0,32},{1,33},{2,34},{3,35},{4,36},{5,37},{6,38},{7,39},{8,40},{9,... | collective-permute-start | bytes 1179656 | tf_op jit(solution)/shard_map/ppermute | solution.py:316
  28.6 8.6 %collective-permute-start.3 = (bf16[512,384]{1,0:T(8,128)(2,1)S(1)}, bf16[512,384]{1,0:T(8,128)(2,1)S(1)}, u32[]{:S(2)}, u32[]{:S(2)}) collective-permute-start(bf16[512,384]{1,0:T(8,128)(2,1)S(1)} %bitcast.9), channel_id=1, source_target_pairs={{0,224},{1,225},{2,226},{3,227},{4,228},{5,229},{6,230},{7,231},{8... | collective-permute-start | bytes 1179656 | tf_op jit(solution)/shard_map/ppermute | solution.py:317
  37.2 3.8 %collective-permute-done.1.refs_1_ = bf16[512,384]{1,0:T(8,128)(2,1)S(1)} collective-permute-done((bf16[512,384]{1,0:T(8,128)(2,1)S(1)}, bf16[512,384]{1,0:T(8,128)(2,1)S(1)}, u32[]{:S(2)}, u32[]{:S(2)}) %collective-permute-start.1) | collective-permute-done | bytes 393248 | tf_op jit(solution)/shard_map/ppermute | solution.py:316
  41.0 1.9 %collective-permute-start.2 = (bf16[512,384]{1,0:T(8,128)(2,1)S(1)}, bf16[512,384]{1,0:T(8,128)(2,1)S(1)}, u32[]{:S(2)}, u32[]{:S(2)}) collective-permute-start(bf16[512,384]{1,0:T(8,128)(2,1)S(1)} %collective-permute-done.1.refs_1_), channel_id=1, source_target_pairs={{0,32},{1,33},{2,34},{3,35},{4,36},{5,37},{6,38},{7,39},{8,40},{9,... | collective-permute-start | bytes 1179656 | tf_op jit(solution)/shard_map/ppermute | solution.py:316
  42.9 1.4 %collective-permute-done.3.refs_2_ = bf16[512,384]{1,0:T(8,128)(2,1)S(1)} collective-permute-done((bf16[512,384]{1,0:T(8,128)(2,1)S(1)}, bf16[512,384]{1,0:T(8,128)(2,1)S(1)}, u32[]{:S(2)}, u32[]{:S(2)}) %collective-permute-start.3) | collective-permute-done | bytes 393248 | tf_op jit(solution)/shard_map/ppermute | solution.py:317
  44.2 5.6 %collective-permute-start.6 = (bf16[512,384]{1,0:T(8,128)(2,1)S(1)}, bf16[512,384]{1,0:T(8,128)(2,1)S(1)}, u32[]{:S(2)}, u32[]{:S(2)}) collective-permute-start(bf16[512,384]{1,0:T(8,128)(2,1)S(1)} %collective-permute-done.3.refs_2_), channel_id=1, source_target_pairs={{0,224},{1,225},{2,226},{3,227},{4,228},{5,229},{6,230},{7,231},{8... | collective-permute-start | bytes 1179656 | tf_op jit(solution)/shard_map/ppermute | solution.py:317
  49.8 0.7 and_select_fusion.order
  50.5 0.0 copy-start.1
  50.5 2.2 %copy-done.1 = bf16[512,4096]{1,0:T(8,128)(2,1)S(1)} copy-done((bf16[512,4096]{1,0:T(8,128)(2,1)S(1)}, bf16[512,4096]{1,0:T(8,128)(2,1)}, u32[]{:S(2)}) %copy-start.1) | copy-done | bytes 4194328
  52.7 1.9 %first.1.refs_7_ = f32[512,384]{1,0:T(8,128)S(1)} custom-call(s32[8]{0:T(128)S(1)} %and_select_fusion.order, bf16[512,384]{1,0:T(8,128)(2,1)S(1)} %bitcast.10, bf16[512,384]{1,0:T(8,128)(2,1)S(1)} %collective-permute-done.1.refs_1_, bf16[512,384]{1,0:T(8,128)(2,1)S(1)} %collective-permute-done.3.refs_2_, bf16[512,4096]{1,0:T(8,128)(2,1)S(1)} %copy-done.1, ...), custom_call_target="tpu_custom_call" | custom-call | flops 603979776 | bytes 2359296 | tf_op jit(solution)/shard_map/first/pallas_call | solution.py:76
  54.6 0.0 collective-permute-done.2.refs_3_
  54.6 1.9 %collective-permute-start.5 = (bf16[512,384]{1,0:T(8,128)(2,1)S(1)}, bf16[512,384]{1,0:T(8,128)(2,1)S(1)}, u32[]{:S(2)}, u32[]{:S(2)}) collective-permute-start(bf16[512,384]{1,0:T(8,128)(2,1)S(1)} %collective-permute-done.2.refs_3_), channel_id=1, source_target_pairs={{0,32},{1,33},{2,34},{3,35},{4,36},{5,37},{6,38},{7,39},{8,40},{9,... | collective-permute-start | bytes 1179656 | tf_op jit(solution)/shard_map/ppermute | solution.py:316
  56.5 0.0 collective-permute-done.6.refs_4_
  56.5 5.4 %collective-permute-start.7 = (bf16[512,384]{1,0:T(8,128)(2,1)S(1)}, bf16[512,384]{1,0:T(8,128)(2,1)S(1)}, u32[]{:S(2)}, u32[]{:S(2)}) collective-permute-start(bf16[512,384]{1,0:T(8,128)(2,1)S(1)} %collective-permute-done.6.refs_4_), channel_id=1, source_target_pairs={{0,224},{1,225},{2,226},{3,227},{4,228},{5,229},{6,230},{7,231},{8... | collective-permute-start | bytes 1179656 | tf_op jit(solution)/shard_map/ppermute | solution.py:317
  62.0 2.9 %collective-permute-start.4 = (bf16[512,384]{1,0:T(8,128)(2,1)S(1)}, bf16[512,384]{1,0:T(8,128)(2,1)S(1)}, u32[]{:S(2)}, u32[]{:S(2)}) collective-permute-start(bf16[512,384]{1,0:T(8,128)(2,1)S(1)} %collective-permute-done.2.refs_3_), channel_id=1, source_target_pairs={{0,64},{1,65},{2,66},{3,67},{4,68},{5,69},{6,70},{7,71},{8,72},{9,... | collective-permute-start | bytes 1179656 | tf_op jit(solution)/shard_map/ppermute | solution.py:326
  64.9 0.1 slice.13.order
  64.9 0.6 slice.12
  65.5 0.7 pad_add_fusion.scalars
  66.2 0.0 collective-permute-done.refs_8_.refs_9_.refs_10_.refs_11_.refs_12_.refs_5_.refs_6_.other
  66.2 4.4 %second.1 = (f32[512,384]{1,0:T(8,128)S(1)}, f32[512,384]{1,0:T(8,128)S(1)}) custom-call(s32[8]{0:T(128)S(1)} %and_select_fusion.order, bf16[512,384]{1,0:T(8,128)(2,1)S(1)} %bitcast.11, bf16[512,384]{1,0:T(8,128)(2,1)S(1)} %collective-permute-done.1.refs_1_, bf16[512,384]{1,0:T(8,128)(2,1)S(1)} %collective-permute-done.3.refs_2_, ...), custom_call_target="tpu_custom_call" | custom-call | flops 1409286144 | bytes 5505024 | tf_op jit(solution)/shard_map/second/pallas_call | solution.py:76
  70.7 0.0 collective-permute-done.5.refs_0_
  70.7 3.1 %collective-permute-done.7.refs_1_ = bf16[512,384]{1,0:T(8,128)(2,1)S(1)} collective-permute-done((bf16[512,384]{1,0:T(8,128)(2,1)S(1)}, bf16[512,384]{1,0:T(8,128)(2,1)S(1)}, u32[]{:S(2)}, u32[]{:S(2)}) %collective-permute-start.7) | collective-permute-done | bytes 393248 | tf_op jit(solution)/shard_map/ppermute | solution.py:317
  73.8 3.2 %third.1 = (f32[512,384]{1,0:T(8,128)S(1)}, f32[512,384]{1,0:T(8,128)S(1)}) custom-call(s32[2]{0:T(128)S(1)} %slice.13.order, bf16[512,384]{1,0:T(8,128)(2,1)S(1)} %collective-permute-done.5.refs_0_, bf16[512,384]{1,0:T(8,128)(2,1)S(1)} %collective-permute-done.7.refs_1_, bf16[512,4096]{1,0:T(8,128)(2,1)} %mine, bf16[512,4096]{1,0:T(8,128)(2,1)} %mine, ...), custom_call_target="tpu_custom_call" | custom-call | flops 805306368 | bytes 3145728 | tf_op jit(solution)/shard_map/third/pallas_call | solution.py:76
  77.1 2.0 %collective-permute-done.4.weight = bf16[512,384]{1,0:T(8,128)(2,1)S(1)} collective-permute-done((bf16[512,384]{1,0:T(8,128)(2,1)S(1)}, bf16[512,384]{1,0:T(8,128)(2,1)S(1)}, u32[]{:S(2)}, u32[]{:S(2)}) %collective-permute-start.4) | collective-permute-done | bytes 393248 | tf_op jit(solution)/shard_map/ppermute | solution.py:326
  79.1 2.6 %finish.1 = (bf16[512,384]{1,0:T(8,128)(2,1)S(1)}, bf16[512,384]{1,0:T(8,128)(2,1)S(1)}) custom-call(s32[2]{0:T(128)S(1)} %pad_add_fusion.scalars, bf16[512,4096]{1,0:T(8,128)(2,1)} %mine, bf16[512,4096]{1,0:T(8,128)(2,1)} %collective-permute-done.refs_8_.refs_9_.refs_10_.refs_11_.refs_12_.refs_5_.refs_6_.other, ...), custom_call_target="tpu_custom_call" | custom-call | flops 402653184 | bytes 2621440 | tf_op jit(solution)/shard_map/finish/pallas_call | solution.py:120
  81.7 1.9 %collective-permute-start.8 = (bf16[512,384]{1,0:T(8,128)(2,1)S(1)}, bf16[512,384]{1,0:T(8,128)(2,1)S(1)}, u32[]{:S(2)}, u32[]{:S(2)}) collective-permute-start(bf16[512,384]{1,0:T(8,128)(2,1)S(1)} %get-tuple-element.31), channel_id=1, source_target_pairs={{0,256},{256,0},{1,257},{257,1},{2,258},{258,2},{3,259},{259,3},{4... | collective-permute-start | bytes 1179656 | tf_op jit(solution)/shard_map/ppermute | solution.py:38
  83.6 1.7 %collective-permute-done.8.q_other = bf16[512,384]{1,0:T(8,128)(2,1)S(1)} collective-permute-done((bf16[512,384]{1,0:T(8,128)(2,1)S(1)}, bf16[512,384]{1,0:T(8,128)(2,1)S(1)}, u32[]{:S(2)}, u32[]{:S(2)}) %collective-permute-start.8) | collective-permute-done | bytes 393248 | tf_op jit(solution)/shard_map/ppermute | solution.py:38
  85.4 4.4 %collective-permute-start.9 = (bf16[512,256]{1,0:T(8,128)(2,1)S(1)}, bf16[512,256]{1,0:T(8,128)(2,1)S(1)}, u32[]{:S(2)}, u32[]{:S(2)}) collective-permute-start(bf16[512,256]{1,0:T(8,128)(2,1)S(1)} %pad_maximum_fusion.2.own), channel_id=1, source_target_pairs={{0,8},{1,9},{2,10},{3,11},{4,12},{5,13},{6,14},{7,15},{8,16},{9,17... | collective-permute-start | bytes 786440 | tf_op jit(solution)/shard_map/ppermute | solution.py:345
  89.8 3.1 %collective-permute-start.11 = (bf16[512,256]{1,0:T(8,128)(2,1)S(1)}, bf16[512,256]{1,0:T(8,128)(2,1)S(1)}, u32[]{:S(2)}, u32[]{:S(2)}) collective-permute-start(bf16[512,256]{1,0:T(8,128)(2,1)S(1)} %pad_maximum_fusion.2.own), channel_id=1, source_target_pairs={{0,24},{1,25},{2,26},{3,27},{4,28},{5,29},{6,30},{7,31},{8,32},{9,... | collective-permute-start | bytes 786440 | tf_op jit(solution)/shard_map/ppermute | solution.py:346
  92.9 10.6 %collective-permute-done.9.one_three = bf16[512,256]{1,0:T(8,128)(2,1)S(1)} collective-permute-done((bf16[512,256]{1,0:T(8,128)(2,1)S(1)}, bf16[512,256]{1,0:T(8,128)(2,1)S(1)}, u32[]{:S(2)}, u32[]{:S(2)}) %collective-permute-start.9) | collective-permute-done | bytes 262176 | tf_op jit(solution)/shard_map/ppermute | solution.py:345
  103.5 1.9 %collective-permute-start.10 = (bf16[512,256]{1,0:T(8,128)(2,1)S(1)}, bf16[512,256]{1,0:T(8,128)(2,1)S(1)}, u32[]{:S(2)}, u32[]{:S(2)}) collective-permute-start(bf16[512,256]{1,0:T(8,128)(2,1)S(1)} %collective-permute-done.9.one_three), channel_id=1, source_target_pairs={{0,8},{1,9},{2,10},{3,11},{4,12},{5,13},{6,14},{7,15},{8,16},{9,17... | collective-permute-start | bytes 786440 | tf_op jit(solution)/shard_map/ppermute | solution.py:347
  105.4 0.1 copy.9.starts
  105.6 0.0 collective-permute-done.11.three_one
  105.6 4.8 %attend_near.1 = (f32[2048,128]{1,0:T(8,128)S(1)}, f32[2048,128]{1,0:T(8,128)S(1)}) custom-call(s32[1]{0:T(128)} %bitcast.core, bf16[512,384]{1,0:T(8,128)(2,1)S(1)} %get-tuple-element.30.q_mine, bf16[512,384]{1,0:T(8,128)(2,1)S(1)} %collective-permute-done.8.q_other, bf16[512,256]{1,0:T(8,128)(2,1)S(1)} %collective-permute-done.9.one_three, ...), custom_call_target="tpu_custom_call" | custom-call | flops 1207959552 | bytes 2097152 | tf_op jit(solution)/shard_map/attend_near/pallas_call | solution.py:252
  110.4 6.4 %collective-permute-done.10.two = bf16[512,256]{1,0:T(8,128)(2,1)S(1)} collective-permute-done((bf16[512,256]{1,0:T(8,128)(2,1)S(1)}, bf16[512,256]{1,0:T(8,128)(2,1)S(1)}, u32[]{:S(2)}, u32[]{:S(2)}) %collective-permute-start.10) | collective-permute-done | bytes 262176 | tf_op jit(solution)/shard_map/ppermute | solution.py:347
  116.8 4.2 %attend_last.1 = bf16[512,512]{1,0:T(8,128)(2,1)} custom-call(s32[1]{0:T(128)} %bitcast.core, bf16[512,384]{1,0:T(8,128)(2,1)S(1)} %get-tuple-element.30.q_mine, bf16[512,384]{1,0:T(8,128)(2,1)S(1)} %collective-permute-done.8.q_other, bf16[512,256]{1,0:T(8,128)(2,1)S(1)} %collective-permute-done.10.two, s32[512,1]{1,0:T(8,128)S(1)} %copy.9.starts, ...), custom_call_target="tpu_custom_call" | custom-call | flops 536870912 | bytes 2097152 | tf_op jit(solution)/shard_map/attend_last/pallas_call | solution.py:267
  (7 shorter events, 0.1 us)
Async XLA Ops:
  0.0 0.9 copy-start
  2.5 19.9 %all-to-all-start = ((bf16[4,128,384]{2,1,0:T(8,128)(2,1)}), bf16[4,128,384]{2,1,0:T(8,128)(2,1)S(1)}, u32[]{:S(2)}, u32[]{:S(2)}) async-start(bf16[4,128,384]{2,1,0:T(8,128)(2,1)} %broadcast_in_dim.22), calls=%async_computation | async-start | bytes 786432 | tf_op jit(solution)/shard_map/all_to_all | solution.py:43
  22.4 43.9 %collective-permute-start = (bf16[512,4096]{1,0:T(8,128)(2,1)}, bf16[512,4096]{1,0:T(8,128)(2,1)}, u32[]{:S(2)}, u32[]{:S(2)}) collective-permute-start(bf16[512,4096]{1,0:T(8,128)(2,1)} %mine), channel_id=1, source_target_pairs={{0,256},{256,0},{1,257},{257,1},{2,258},{258,2},{3,259},{259,3},{4... | collective-permute-start | bytes 12582920 | tf_op jit(solution)/shard_map/ppermute | solution.py:38
  24.3 16.7 %collective-permute-start.1 = (bf16[512,384]{1,0:T(8,128)(2,1)S(1)}, bf16[512,384]{1,0:T(8,128)(2,1)S(1)}, u32[]{:S(2)}, u32[]{:S(2)}) collective-permute-start(bf16[512,384]{1,0:T(8,128)(2,1)S(1)} %bitcast.8), channel_id=1, source_target_pairs={{0,32},{1,33},{2,34},{3,35},{4,36},{5,37},{6,38},{7,39},{8,40},{9,... | collective-permute-start | bytes 1179656 | tf_op jit(solution)/shard_map/ppermute | solution.py:316
  28.6 15.7 %collective-permute-start.3 = (bf16[512,384]{1,0:T(8,128)(2,1)S(1)}, bf16[512,384]{1,0:T(8,128)(2,1)S(1)}, u32[]{:S(2)}, u32[]{:S(2)}) collective-permute-start(bf16[512,384]{1,0:T(8,128)(2,1)S(1)} %bitcast.9), channel_id=1, source_target_pairs={{0,224},{1,225},{2,226},{3,227},{4,228},{5,229},{6,230},{7,231},{8... | collective-permute-start | bytes 1179656 | tf_op jit(solution)/shard_map/ppermute | solution.py:317
  41.0 13.6 %collective-permute-start.2 = (bf16[512,384]{1,0:T(8,128)(2,1)S(1)}, bf16[512,384]{1,0:T(8,128)(2,1)S(1)}, u32[]{:S(2)}, u32[]{:S(2)}) collective-permute-start(bf16[512,384]{1,0:T(8,128)(2,1)S(1)} %collective-permute-done.1.refs_1_), channel_id=1, source_target_pairs={{0,32},{1,33},{2,34},{3,35},{4,36},{5,37},{6,38},{7,39},{8,40},{9,... | collective-permute-start | bytes 1179656 | tf_op jit(solution)/shard_map/ppermute | solution.py:316
  44.2 12.3 %collective-permute-start.6 = (bf16[512,384]{1,0:T(8,128)(2,1)S(1)}, bf16[512,384]{1,0:T(8,128)(2,1)S(1)}, u32[]{:S(2)}, u32[]{:S(2)}) collective-permute-start(bf16[512,384]{1,0:T(8,128)(2,1)S(1)} %collective-permute-done.3.refs_2_), channel_id=1, source_target_pairs={{0,224},{1,225},{2,226},{3,227},{4,228},{5,229},{6,230},{7,231},{8... | collective-permute-start | bytes 1179656 | tf_op jit(solution)/shard_map/ppermute | solution.py:317
  50.5 2.2 %copy-start.1 = (bf16[512,4096]{1,0:T(8,128)(2,1)S(1)}, bf16[512,4096]{1,0:T(8,128)(2,1)}, u32[]{:S(2)}) copy-start(bf16[512,4096]{1,0:T(8,128)(2,1)} %mine) | copy-start | bytes 12582916
  54.6 16.1 %collective-permute-start.5 = (bf16[512,384]{1,0:T(8,128)(2,1)S(1)}, bf16[512,384]{1,0:T(8,128)(2,1)S(1)}, u32[]{:S(2)}, u32[]{:S(2)}) collective-permute-start(bf16[512,384]{1,0:T(8,128)(2,1)S(1)} %collective-permute-done.2.refs_3_), channel_id=1, source_target_pairs={{0,32},{1,33},{2,34},{3,35},{4,36},{5,37},{6,38},{7,39},{8,40},{9,... | collective-permute-start | bytes 1179656 | tf_op jit(solution)/shard_map/ppermute | solution.py:316
  56.5 17.3 %collective-permute-start.7 = (bf16[512,384]{1,0:T(8,128)(2,1)S(1)}, bf16[512,384]{1,0:T(8,128)(2,1)S(1)}, u32[]{:S(2)}, u32[]{:S(2)}) collective-permute-start(bf16[512,384]{1,0:T(8,128)(2,1)S(1)} %collective-permute-done.6.refs_4_), channel_id=1, source_target_pairs={{0,224},{1,225},{2,226},{3,227},{4,228},{5,229},{6,230},{7,231},{8... | collective-permute-start | bytes 1179656 | tf_op jit(solution)/shard_map/ppermute | solution.py:317
  62.0 17.1 %collective-permute-start.4 = (bf16[512,384]{1,0:T(8,128)(2,1)S(1)}, bf16[512,384]{1,0:T(8,128)(2,1)S(1)}, u32[]{:S(2)}, u32[]{:S(2)}) collective-permute-start(bf16[512,384]{1,0:T(8,128)(2,1)S(1)} %collective-permute-done.2.refs_3_), channel_id=1, source_target_pairs={{0,64},{1,65},{2,66},{3,67},{4,68},{5,69},{6,70},{7,71},{8,72},{9,... | collective-permute-start | bytes 1179656 | tf_op jit(solution)/shard_map/ppermute | solution.py:326
  81.7 3.6 %collective-permute-start.8 = (bf16[512,384]{1,0:T(8,128)(2,1)S(1)}, bf16[512,384]{1,0:T(8,128)(2,1)S(1)}, u32[]{:S(2)}, u32[]{:S(2)}) collective-permute-start(bf16[512,384]{1,0:T(8,128)(2,1)S(1)} %get-tuple-element.31), channel_id=1, source_target_pairs={{0,256},{256,0},{1,257},{257,1},{2,258},{258,2},{3,259},{259,3},{4... | collective-permute-start | bytes 1179656 | tf_op jit(solution)/shard_map/ppermute | solution.py:38
  85.4 18.1 %collective-permute-start.9 = (bf16[512,256]{1,0:T(8,128)(2,1)S(1)}, bf16[512,256]{1,0:T(8,128)(2,1)S(1)}, u32[]{:S(2)}, u32[]{:S(2)}) collective-permute-start(bf16[512,256]{1,0:T(8,128)(2,1)S(1)} %pad_maximum_fusion.2.own), channel_id=1, source_target_pairs={{0,8},{1,9},{2,10},{3,11},{4,12},{5,13},{6,14},{7,15},{8,16},{9,17... | collective-permute-start | bytes 786440 | tf_op jit(solution)/shard_map/ppermute | solution.py:345
  89.8 15.8 %collective-permute-start.11 = (bf16[512,256]{1,0:T(8,128)(2,1)S(1)}, bf16[512,256]{1,0:T(8,128)(2,1)S(1)}, u32[]{:S(2)}, u32[]{:S(2)}) collective-permute-start(bf16[512,256]{1,0:T(8,128)(2,1)S(1)} %pad_maximum_fusion.2.own), channel_id=1, source_target_pairs={{0,24},{1,25},{2,26},{3,27},{4,28},{5,29},{6,30},{7,31},{8,32},{9,... | collective-permute-start | bytes 786440 | tf_op jit(solution)/shard_map/ppermute | solution.py:346
  103.5 13.3 %collective-permute-start.10 = (bf16[512,256]{1,0:T(8,128)(2,1)S(1)}, bf16[512,256]{1,0:T(8,128)(2,1)S(1)}, u32[]{:S(2)}, u32[]{:S(2)}) collective-permute-start(bf16[512,256]{1,0:T(8,128)(2,1)S(1)} %collective-permute-done.9.one_three), channel_id=1, source_target_pairs={{0,8},{1,9},{2,10},{3,11},{4,12},{5,13},{6,14},{7,15},{8,16},{9,17... | collective-permute-start | bytes 786440 | tf_op jit(solution)/shard_map/ppermute | solution.py:347
